TPU v7x, 512 devices: a whole 4x8x8 slice. The times are simulated.
512 devices in a mesh: tile: 128 (over z, y, core), filt: 4 (over x).
Axes of the slice: x: 4, y: 8, z: 8, core: 2. Of those that a mesh axis runs over, the one named last changes fastest.
Arguments:
- activations: bfloat16 [128, 2, 8, 8, 256], P('tile', None, None, None, 'filt'), may hold values from -6 to 6
- out_grad: bfloat16 [128, 2, 8, 8, 512], P('tile', None, None, None, 'filt'), may hold values from -6 to 6
- kernel: bfloat16 [3, 3, 3, 256, 512], P(None, None, None, None, 'filt'), may hold values from -0.078125 to 0.078125
Outputs:
- input_grad: bfloat16 [128, 2, 8, 8, 256], P('tile', None, None, None, 'filt')
- weight_grad: bfloat16 [3, 3, 3, 256, 512], P(None, None, None, None, 'filt')
All inputs are finite; a program needn't handle non-finite values.
Results may differ from a plain program's by a relative error of at most 0.0015.
Values may be sent and summed in bfloat16 or wider, within the bound.
No kernel may reach another device: no remote copies, remote signals or barrier semaphores. Data moves between devices by JAX's collectives and lax.ppermute only.
A program may use at most 128 MiB of HBM per device.

v0:
```python
import math

import jax
import jax.numpy as jnp
from jax import lax
from jax.sharding import PartitionSpec as P

CLIPS = 2


def from_behind(block, axis, distance):
    devices = range(lax.axis_size(axis))
    route = [(i - distance, i) for i in devices if i - distance in devices]
    return lax.ppermute(block, axis, route)


def spread(block, across, col, row, across_rows):
    west = from_behind(block[:, :, -1:, :], "tile", CLIPS)
    west = jnp.where(col > 0, west, jnp.zeros_like(west))
    east = from_behind(block[:, :, :1, :], "tile", -CLIPS)
    east = jnp.where(col < across - 1, east, jnp.zeros_like(east))
    widened = jnp.concatenate([west, block, east], axis=2)
    north = from_behind(widened[:, -1:, :, :], "tile", CLIPS * across)
    north = jnp.where(row > 0, north, jnp.zeros_like(north))
    south = from_behind(widened[:, :1, :, :], "tile", -CLIPS * across)
    south = jnp.where(row < across_rows - 1, south, jnp.zeros_like(south))
    taller = jnp.concatenate([north, widened, south], axis=1)
    return jnp.pad(taller, ((1, 1), (0, 0), (0, 0), (0, 0)))


def shards(activations, out_grad, kernel):
    tiles = lax.axis_size("tile")
    across = min(8, tiles // CLIPS)
    across_rows = tiles // (CLIPS * across)
    where = lax.axis_index("tile")
    col = where // CLIPS % across
    row = where // (CLIPS * across)
    frames = activations.shape[1]
    height = activations.shape[2]
    width = activations.shape[3]
    cout_local = out_grad.shape[4]
    cin_all = kernel.shape[3]
    count = frames * height * width
    whole = lax.all_gather(activations[0], "filt", axis=3, tiled=True)
    xext = spread(whole, across, col, row, across_rows)
    gext = spread(out_grad[0], across, col, row, across_rows)
    grows = out_grad[0].reshape(count, cout_local)
    gcols = []
    for ta in range(3):
        for tb in range(3):
            for te in range(3):
                gcols.append(
                    gext[
                        2 - ta : 2 - ta + frames,
                        2 - tb : 2 - tb + height,
                        2 - te : 2 - te + width,
                        :,
                    ].reshape(count, cout_local)
                )
    gstack = jnp.stack(gcols, axis=1)
    kernel_flat = kernel.reshape(27, cin_all, cout_local)
    terms = lax.dot_general(
        gstack, kernel_flat, (((1, 2), (0, 2)), ((), ())), preferred_element_type=jnp.float32
    )
    terms = terms.reshape(1, frames, height, width, cin_all)
    input_grad = lax.psum_scatter(terms, "filt", scatter_dimension=4, tiled=True).astype(
        jnp.bfloat16
    )
    scale = 1.0 / math.sqrt(tiles * count)

    def frame_tap(ta):
        xcols = []
        for tb in range(3):
            for te in range(3):
                xcols.append(
                    xext[ta : ta + frames, tb : tb + height, te : te + width, :].reshape(
                        count, cin_all
                    )
                )
        xstack = jnp.stack(xcols, axis=1)
        return lax.dot_general(
            xstack, grows, (((0,), (0,)), ((), ())), preferred_element_type=jnp.float32
        )

    local = jnp.concatenate([frame_tap(ta) for ta in range(3)], axis=0)
    summed = lax.psum(local, "tile")
    weight_grad = (summed.reshape(3, 3, 3, cin_all, cout_local) * scale).astype(jnp.bfloat16)
    return (input_grad, weight_grad)


def solution(mesh):
    in_specs = (
        P("tile", None, None, None, "filt"),
        P("tile", None, None, None, "filt"),
        P(None, None, None, None, "filt"),
    )
    out_specs = (P("tile", None, None, None, "filt"), P(None, None, None, None, "filt"))
    return jax.shard_map(shards, mesh=mesh, in_specs=in_specs, out_specs=out_specs, check_vma=False)
```

profile of v0, /device:TPU:1, one launch (start us, length us, event | category | flops | bytes accessed | tf_op | source)
XLA Modules:
  0.0 329.5 jit_solution(11987457850489722794)
XLA Ops:
  8.1 0.9 fusion.19
  9.0 4.0 %collective-permute-start = (bf16[2,8,1,128]{3,2,1,0:T(2,128)(2,1)S(1)}, bf16[2,8,1,128]{3,2,1,0:T(2,128)(2,1)S(1)}, u32[]{:S(2)}, u32[]{:S(2)}) collective-permute-start(bf16[2,8,1,128]{3,2,1,0:T(2,128)(2,1)S(1)} %get-tuple-element.38), channel_id=1, source_target_pairs={{0,8},{4,12},{8,16},{12,20},{16,24},{20,28},{24,32},{28,36},{32,40... | collective-permute-start | bytes 12296 | tf_op jit(solution)/shard_map/ppermute | solution.py:14
  13.0 1.0 copy.134
  14.0 13.6 %all-gather = bf16[1,2,8,8,256]{3,2,1,0,4:T(8,128)(2,1)S(1)} all-gather(bf16[1,2,8,8,64]{3,2,1,0,4:T(8,128)(2,1)S(1)} %copy.134), channel_id=2, replica_groups=mesh['tile'=128,'filt'=4] {'filt'}, dimensions={4}, use_global_device_ids=true | all-gather | bytes 81920 | tf_op jit(solution)/shard_map/all_gather | solution.py:44
  28.5 1.3 collective-permute-start.5
  29.8 4.0 %collective-permute-start.4 = (bf16[2,8,1,256]{3,2,1,0:T(2,128)(2,1)S(1)}, bf16[2,8,1,256]{3,2,1,0:T(2,128)(2,1)S(1)}, u32[]{:S(2)}, u32[]{:S(2)}) collective-permute-start(bf16[2,8,1,256]{3,2,1,0:T(2,128)(2,1)S(1)} %get-tuple-element.32), channel_id=1, source_target_pairs={{0,8},{4,12},{8,16},{12,20},{16,24},{20,28},{24,32},{28,36},{32,40... | collective-permute-start | bytes 24584 | tf_op jit(solution)/shard_map/ppermute | solution.py:14
  33.8 1.3 collective-permute-start.1
  35.9 2.3 collective-permute-done.1
  38.3 6.5 %collective-permute-start.2 = (bf16[2,1,10,128]{3,2,1,0:T(8,128)(2,1)S(1)}, bf16[2,1,10,128]{3,2,1,0:T(8,128)(2,1)S(1)}, u32[]{:S(2)}, u32[]{:S(2)}) collective-permute-start(bf16[2,1,10,128]{3,2,1,0:T(8,128)(2,1)S(1)} %get-tuple-element.36), channel_id=1, source_target_pairs={{0,64},{4,68},{8,72},{12,76},{16,80},{20,84},{24,88},{28,92},{32,9... | collective-permute-start | bytes 15368 | tf_op jit(solution)/shard_map/ppermute | solution.py:14
  44.7 1.3 collective-permute-start.3
  46.2 1.3 collective-permute-start.7
  47.5 5.3 %collective-permute-start.6 = (bf16[2,1,10,256]{3,2,1,0:T(8,128)(2,1)S(1)}, bf16[2,1,10,256]{3,2,1,0:T(8,128)(2,1)S(1)}, u32[]{:S(2)}, u32[]{:S(2)}) collective-permute-start(bf16[2,1,10,256]{3,2,1,0:T(8,128)(2,1)S(1)} %get-tuple-element.28), channel_id=1, source_target_pairs={{0,64},{4,68},{8,72},{12,76},{16,80},{20,84},{24,88},{28,92},{32,9... | collective-permute-start | bytes 30728 | tf_op jit(solution)/shard_map/ppermute | solution.py:14
  55.8 2.4 copy.166
  58.2 3.2 reshape.79
  64.1 1.6 copy.137
  65.7 1.6 copy.138
  67.3 1.6 copy.139
  68.8 1.6 copy.140
  74.0 1.0 copy.146
  75.6 1.6 copy.147
  80.1 0.9 constant_dynamic-update-slice_fusion.34
  81.9 0.9 constant_dynamic-update-slice_fusion.32
  86.3 1.4 fusion.20
  90.3 1.3 fusion.21
  91.6 1.6 copy.155
  93.2 1.5 constant_dynamic-update-slice_fusion.53
  96.3 1.6 constant_dynamic-update-slice_fusion.52
  102.2 1.3 fusion.22
  103.6 2.2 pad_maximum_fusion
  105.8 1.1 reshape.80
  107.7 210.7 %all-reduce.4.cloned.1.call-done = f32[27,256,128]{2,1,0:T(8,128)} async-done(((f32[27,256,128]{2,1,0:T(8,128)}), f32[27,256,128]{2,1,0:T(8,128)}) %all-reduce.4.cloned.1.call-update) | async-done | bytes 3538960 | tf_op jit(solution)/shard_map/psum | solution.py:86
  318.5 3.6 %multiply_convert_fusion = bf16[27,256,128]{2,1,0:T(8,128)(2,1)} fusion(f32[27,256,128]{2,1,0:T(8,128)} %all-reduce.4.cloned.1.call-done), kind=kLoop, calls=%fused_computation.1 | loop fusion | flops 1769472 | bytes 5308416 | tf_op jit(solution)/shard_map/convert_element_type | solution.py:87
  (127 shorter events, 28.3 us)
Async XLA Ops:
  8.0 47.1 %copy-start = (bf16[3,3,3,256,128]{4,3,2,1,0:T(8,128)(2,1)S(1)}, bf16[3,3,3,256,128]{4,3,2,1,0:T(8,128)(2,1)}, u32[]{:S(2)}) copy-start(bf16[3,3,3,256,128]{4,3,2,1,0:T(8,128)(2,1)} %param.5) | copy-start | bytes 5308420
  8.0 30.2 %copy-start.2 = (bf16[1,2,8,8,128]{4,3,2,1,0:T(8,128)(2,1)S(1)}, bf16[1,2,8,8,128]{4,3,2,1,0:T(8,128)(2,1)}, u32[]{:S(2)}) copy-start(bf16[1,2,8,8,128]{4,3,2,1,0:T(8,128)(2,1)} %param.4) | copy-start | bytes 98308
  8.0 97.8 %reduce-scatter.4.cloned.1.call-start = ((), (), s32[]{:S(2)}) async-start(), calls=%async_computation.2 | async-start | bytes 163840
  9.0 26.9 %collective-permute-start = (bf16[2,8,1,128]{3,2,1,0:T(2,128)(2,1)S(1)}, bf16[2,8,1,128]{3,2,1,0:T(2,128)(2,1)S(1)}, u32[]{:S(2)}, u32[]{:S(2)}) collective-permute-start(bf16[2,8,1,128]{3,2,1,0:T(2,128)(2,1)S(1)} %get-tuple-element.38), channel_id=1, source_target_pairs={{0,8},{4,12},{8,16},{12,20},{16,24},{20,28},{24,32},{28,36},{32,40... | collective-permute-start | bytes 12296 | tf_op jit(solution)/shard_map/ppermute | solution.py:14
  28.5 17.5 %collective-permute-start.5 = (bf16[2,8,1,256]{3,2,1,0:T(2,128)(2,1)S(1)}, bf16[2,8,1,256]{3,2,1,0:T(2,128)(2,1)S(1)}, u32[]{:S(2)}, u32[]{:S(2)}) collective-permute-start(bf16[2,8,1,256]{3,2,1,0:T(2,128)(2,1)S(1)} %get-tuple-element.33), channel_id=1, source_target_pairs={{8,0},{12,4},{16,8},{20,12},{24,16},{28,20},{32,24},{36,28},{40,32... | collective-permute-start | bytes 24584 | tf_op jit(solution)/shard_map/ppermute | solution.py:14
  29.8 16.2 %collective-permute-start.4 = (bf16[2,8,1,256]{3,2,1,0:T(2,128)(2,1)S(1)}, bf16[2,8,1,256]{3,2,1,0:T(2,128)(2,1)S(1)}, u32[]{:S(2)}, u32[]{:S(2)}) collective-permute-start(bf16[2,8,1,256]{3,2,1,0:T(2,128)(2,1)S(1)} %get-tuple-element.32), channel_id=1, source_target_pairs={{0,8},{4,12},{8,16},{12,20},{16,24},{20,28},{24,32},{28,36},{32,40... | collective-permute-start | bytes 24584 | tf_op jit(solution)/shard_map/ppermute | solution.py:14
  33.8 4.4 %collective-permute-start.1 = (bf16[2,8,1,128]{3,2,1,0:T(2,128)(2,1)S(1)}, bf16[2,8,1,128]{3,2,1,0:T(2,128)(2,1)S(1)}, u32[]{:S(2)}, u32[]{:S(2)}) collective-permute-start(bf16[2,8,1,128]{3,2,1,0:T(2,128)(2,1)S(1)} %get-tuple-element.39), channel_id=1, source_target_pairs={{8,0},{12,4},{16,8},{20,12},{24,16},{28,20},{32,24},{36,28},{40,32... | collective-permute-start | bytes 12296 | tf_op jit(solution)/shard_map/ppermute | solution.py:14
  38.3 16.0 %collective-permute-start.2 = (bf16[2,1,10,128]{3,2,1,0:T(8,128)(2,1)S(1)}, bf16[2,1,10,128]{3,2,1,0:T(8,128)(2,1)S(1)}, u32[]{:S(2)}, u32[]{:S(2)}) collective-permute-start(bf16[2,1,10,128]{3,2,1,0:T(8,128)(2,1)S(1)} %get-tuple-element.36), channel_id=1, source_target_pairs={{0,64},{4,68},{8,72},{12,76},{16,80},{20,84},{24,88},{28,92},{32,9... | collective-permute-start | bytes 15368 | tf_op jit(solution)/shard_map/ppermute | solution.py:14
  44.7 9.5 %collective-permute-start.3 = (bf16[2,1,10,128]{3,2,1,0:T(8,128)(2,1)S(1)}, bf16[2,1,10,128]{3,2,1,0:T(8,128)(2,1)S(1)}, u32[]{:S(2)}, u32[]{:S(2)}) collective-permute-start(bf16[2,1,10,128]{3,2,1,0:T(8,128)(2,1)S(1)} %get-tuple-element.37), channel_id=1, source_target_pairs={{64,0},{68,4},{72,8},{76,12},{80,16},{84,20},{88,24},{92,28},{96,3... | collective-permute-start | bytes 15368 | tf_op jit(solution)/shard_map/ppermute | solution.py:14
  46.2 15.3 %collective-permute-start.7 = (bf16[2,1,10,256]{3,2,1,0:T(8,128)(2,1)S(1)}, bf16[2,1,10,256]{3,2,1,0:T(8,128)(2,1)S(1)}, u32[]{:S(2)}, u32[]{:S(2)}) collective-permute-start(bf16[2,1,10,256]{3,2,1,0:T(8,128)(2,1)S(1)} %get-tuple-element.29), channel_id=1, source_target_pairs={{64,0},{68,4},{72,8},{76,12},{80,16},{84,20},{88,24},{92,28},{96,3... | collective-permute-start | bytes 30728 | tf_op jit(solution)/shard_map/ppermute | solution.py:14
  47.5 14.0 %collective-permute-start.6 = (bf16[2,1,10,256]{3,2,1,0:T(8,128)(2,1)S(1)}, bf16[2,1,10,256]{3,2,1,0:T(8,128)(2,1)S(1)}, u32[]{:S(2)}, u32[]{:S(2)}) collective-permute-start(bf16[2,1,10,256]{3,2,1,0:T(8,128)(2,1)S(1)} %get-tuple-element.28), channel_id=1, source_target_pairs={{0,64},{4,68},{8,72},{12,76},{16,80},{20,84},{24,88},{28,92},{32,9... | collective-permute-start | bytes 30728 | tf_op jit(solution)/shard_map/ppermute | solution.py:14
  61.5 257.0 %all-reduce.4.cloned.1.call-start = ((), (), s32[]{:S(2)}) async-start(), calls=%async_computation.1 | async-start | bytes 7077888 | tf_op jit(solution)/shard_map/psum | solution.py:86
  74.0 11.4 %copy-start.9 = (bf16[128,1,256]{0,2,1:T(8,128)(2,1)S(1)}, bf16[128,1,256]{0,2,1:T(8,128)(2,1)}, u32[]{:S(2)}) copy-start(bf16[128,1,256]{0,2,1:T(8,128)(2,1)} %copy.143) | copy-start | bytes 196612
  74.0 11.4 %copy-start.7 = (bf16[128,1,256]{0,2,1:T(8,128)(2,1)S(1)}, bf16[128,1,256]{0,2,1:T(8,128)(2,1)}, u32[]{:S(2)}) copy-start(bf16[128,1,256]{0,2,1:T(8,128)(2,1)} %copy.144) | copy-start | bytes 196612
  80.1 7.5 %copy-start.4 = (bf16[128,9,256]{0,2,1:T(8,128)(2,1)S(1)}, bf16[128,9,256]{0,2,1:T(8,128)(2,1)}, u32[]{:S(2)}) copy-start(bf16[128,9,256]{0,2,1:T(8,128)(2,1)} %constant_dynamic-update-slice_fusion.44) | copy-start | bytes 1769476
  80.1 7.5 %copy-start.10 = (bf16[128,1,256]{0,2,1:T(8,128)(2,1)S(1)}, bf16[128,1,256]{0,2,1:T(8,128)(2,1)}, u32[]{:S(2)}) copy-start(bf16[128,1,256]{0,2,1:T(8,128)(2,1)} %copy.147) | copy-start | bytes 196612
  80.1 7.6 %copy-start.11 = (bf16[128,1,256]{0,2,1:T(8,128)(2,1)S(1)}, bf16[128,1,256]{0,2,1:T(8,128)(2,1)}, u32[]{:S(2)}) copy-start(bf16[128,1,256]{0,2,1:T(8,128)(2,1)} %copy.148) | copy-start | bytes 196612
  80.1 10.2 %copy-start.8 = (bf16[128,1,256]{0,2,1:T(8,128)(2,1)S(1)}, bf16[128,1,256]{0,2,1:T(8,128)(2,1)}, u32[]{:S(2)}) copy-start(bf16[128,1,256]{0,2,1:T(8,128)(2,1)} %copy.152) | copy-start | bytes 196612
  81.0 9.3 %copy-start.5 = (bf16[128,1,256]{0,2,1:T(8,128)(2,1)S(1)}, bf16[128,1,256]{0,2,1:T(8,128)(2,1)}, u32[]{:S(2)}) copy-start(bf16[128,1,256]{0,2,1:T(8,128)(2,1)} %copy.153) | copy-start | bytes 196612
  81.9 8.4 %copy-start.6 = (bf16[128,1,256]{0,2,1:T(8,128)(2,1)S(1)}, bf16[128,1,256]{0,2,1:T(8,128)(2,1)}, u32[]{:S(2)}) copy-start(bf16[128,1,256]{0,2,1:T(8,128)(2,1)} %copy.154) | copy-start | bytes 196612
  85.4 0.8 copy-start.3
  96.2 7.3 %copy-start.1 = (f32[9,256,128]{2,1,0:T(8,128)S(1)}, f32[9,256,128]{2,1,0:T(8,128)}, u32[]{:S(2)}) copy-start(f32[9,256,128]{2,1,0:T(8,128)} %fusion.21) | copy-start | bytes 3538948
Sparse Core Ops, SparseCore 0:
  61.6 32.4 reduce-scatter.3
Sparse Core Ops, SparseCore 1:
  105.8 212.6 all-reduce.3
where the time goes:
time: 332 us; the launch traced here: 330 us
  waiting for transfers between devices  213 us (64%)
  local copies, waits for them, and re-layouts  50.6 us (15%)
  starting transfers between devices  25 us (8%)
  between operations  16.1 us (5%)
  blocking collectives  13.6 us (4%)
  other arithmetic  6.39 us (2%)
  matrix products  4.73 us (1%)
    psum x1, waiting for transfers between devices, shards(): summed = lax.psum(local, 'tile')  211 us
    unnamed x77, local copies, waits for them, and re-layouts  26.1 us
    ppermute x8, starting transfers between devices, from_behind(): return lax.ppermute(block, axis, route)  24.9 us
    another operation x30, local copies, waits for them, and re-layouts, frame_tap(): xstack = jnp.stack(xcols, axis=1)  21.2 us
    all_gather x1, blocking collectives, shards(): whole = lax.all_gather(activations[0], 'filt', axis=3, tiled=True)  13.6 us
  transfers between devices with their start and end apart: 10, of which 2 were waited for; matrix products, arithmetic and copies ran while one was open for 17% of the time, Pallas kernels for 0%

commit v1 on v0

v1 whole, which is shorter than its diff:
```python
import math

import jax
import jax.numpy as jnp
from jax import lax
from jax.experimental import pallas as pl
from jax.experimental.pallas import tpu as pltpu
from jax.sharding import Mesh
from jax.sharding import PartitionSpec as P

AXES = ("z", "y", "core", "x")
TILE = ("z", "y", "core")
NZ, NY, NC, NX = 8, 8, 2, 4
F, H, W = 2, 8, 8
CIN, COUT = 256, 512
CI, CO = CIN // NX, COUT // NX
GROWS = F * (H + 2) * W
CJ = CI // NY
XROWS = 16
CHUNK = 7 * CJ


def tile_index(z, y, core):
    return (z * NY + y) * NC + core


SPARSE = [
    [tile_index(a + 2 * i, b + 2 * j, c) for i in range(4) for j in range(4)]
    for a in range(2)
    for b in range(2)
    for c in range(NC)
]
BLOCKS = [
    [tile_index(2 * i + a, 2 * j + b, c) for a in range(2) for b in range(2)]
    for i in range(4)
    for j in range(4)
    for c in range(NC)
]


def shifted(own, left, right, tap):
    if tap == 1:
        return own
    row = lax.broadcasted_iota(jnp.int32, own.shape, own.ndim - 2)
    axis = own.ndim - 2
    if tap == 0:
        return jnp.where(row == W - 1, pltpu.roll(right, W - 1, axis), pltpu.roll(own, W - 1, axis))
    return jnp.where(row == 0, pltpu.roll(left, 1, axis), pltpu.roll(own, 1, axis))


def input_kernel(col_ref, g_ref, k_ref, out_ref):
    col = col_ref[0]

    def tile(i):
        return g_ref[i, :GROWS, :].astype(jnp.float32).reshape(F * (H + 2), W, CO)

    own = tile(col)
    left = jnp.where(col > 0, tile(jnp.maximum(col - 1, 0)), 0.0)
    right = jnp.where(col < NY - 1, tile(jnp.minimum(col + 1, NY - 1)), 0.0)
    acc0 = jnp.zeros((H * W, CIN), jnp.float32)
    acc1 = jnp.zeros((H * W, CIN), jnp.float32)
    dims = (((1,), (1,)), ((), ()))
    for te in range(3):
        moved = shifted(own, left, right, te).reshape(F, H + 2, W, CO)
        for tb in range(3):
            rows = moved[:, 2 - tb : 2 - tb + H].reshape(F, H * W, CO).astype(jnp.bfloat16)
            both = jnp.concatenate([rows[0], rows[1]], axis=1)
            k0, k1, k2 = (k_ref[ta * 9 + tb * 3 + te] for ta in range(3))
            acc0 += lax.dot_general(
                both, jnp.concatenate([k1, k0], axis=1), dims, preferred_element_type=jnp.float32
            )
            acc1 += lax.dot_general(
                both, jnp.concatenate([k2, k1], axis=1), dims, preferred_element_type=jnp.float32
            )
    for i in range(NX):
        cut = slice(i * CI, (i + 1) * CI)
        out_ref[i] = jnp.concatenate([acc0[:, cut], acc1[:, cut]], axis=1)


def weight_kernel(g_ref, x_ref, out_ref):
    own = g_ref[:, :GROWS, :].astype(jnp.float32).reshape(NY, F * (H + 2), W, CO)
    edge = jnp.zeros((1, F * (H + 2), W, CO), jnp.float32)
    left = jnp.concatenate([edge, own[:-1]], axis=0)
    right = jnp.concatenate([own[1:], edge], axis=0)
    x = x_ref[...].reshape(NX, NY, CJ, F * H * W)
    frames = []
    for f in range(F):
        cut = slice(f * H * W, (f + 1) * H * W)
        cols = [x[:, y, :, cut].reshape(NX * CJ, H * W) for y in range(NY)]
        frames.append(jnp.concatenate(cols, axis=1))
    xs = jnp.concatenate(frames, axis=0).astype(jnp.bfloat16)
    half = NX * CJ
    for te in range(3):
        moved = shifted(own, left, right, te).reshape(NY, F, H + 2, W, CO)
        for tb in range(3):
            rows = moved[:, :, 2 - tb : 2 - tb + H].astype(jnp.bfloat16)
            g0 = rows[:, 0].reshape(NY * H * W, CO)
            g1 = rows[:, 1].reshape(NY * H * W, CO)
            both = jnp.concatenate([g0, g1], axis=1)
            prod = jnp.dot(xs, both, preferred_element_type=jnp.float32)
            parts = (
                prod[:half, CO:],
                prod[:half, :CO] + prod[half:, CO:],
                prod[half:, :CO],
            )
            for ta in range(3):
                group, t = divmod(ta * 9 + tb * 3 + te, 7)
                for q in range(NX):
                    out_ref[(group // 2) * 8 + q * 2 + group % 2, t * CJ : (t + 1) * CJ, :] = parts[
                        ta
                    ][q * CJ : (q + 1) * CJ]
    for q in range(NX):
        out_ref[8 + q * 2 + 1, 6 * CJ : 7 * CJ, :] = jnp.zeros((CJ, CO), jnp.float32)


def shards(activations, out_grad, kernel):
    col = lax.axis_index("y")
    core = lax.axis_index("core")
    g = out_grad[0]
    with jax.named_scope("halo"):
        north = lax.ppermute(g[:, -1:], "z", [(i, i + 1) for i in range(NZ - 1)])
        south = lax.ppermute(g[:, :1], "z", [(i + 1, i) for i in range(NZ - 1)])
        tall = jnp.concatenate([north, g, south], axis=1).reshape(GROWS, CO)
    with jax.named_scope("strip"):
        xt = activations[0].reshape(F * H * W, CI).T.reshape(NY, CJ, F * H * W)
        xt = jnp.pad(xt, ((0, 0), (0, XROWS - CJ), (0, 0)))
        send = jnp.concatenate([jnp.broadcast_to(tall, (NY, GROWS, CO)), xt], axis=1)
        strip = lax.all_to_all(send, "y", 0, 0, tiled=True)
    with jax.named_scope("input_part"):
        terms = pl.pallas_call(
            input_kernel,
            out_shape=jax.ShapeDtypeStruct((NX, H * W, F * CI), jnp.float32),
            in_specs=[
                pl.BlockSpec(memory_space=pltpu.SMEM),
                pl.BlockSpec(memory_space=pltpu.VMEM),
                pl.BlockSpec(memory_space=pltpu.VMEM),
            ],
            out_specs=pl.BlockSpec(memory_space=pltpu.VMEM),
            compiler_params=pltpu.CompilerParams(vmem_limit_bytes=32 * 1024 * 1024),
        )(col.reshape(1).astype(jnp.int32), strip, kernel.reshape(27, CIN, CO))
    with jax.named_scope("filters"):
        xmine = strip[:, GROWS : GROWS + CJ].reshape(NY * CJ, F * H * W).astype(jnp.float32)
        send = jnp.concatenate([terms, jnp.broadcast_to(xmine, (NX,) + xmine.shape)], axis=1)
        got = lax.all_to_all(send, "x", 0, 0, tiled=True)
    with jax.named_scope("weight_part"):
        local = pl.pallas_call(
            weight_kernel,
            out_shape=jax.ShapeDtypeStruct((NZ * NC, CHUNK, CO), jnp.float32),
            in_specs=[pl.BlockSpec(memory_space=pltpu.VMEM)] * 2,
            out_specs=pl.BlockSpec(memory_space=pltpu.VMEM),
            compiler_params=pltpu.CompilerParams(vmem_limit_bytes=32 * 1024 * 1024),
        )(strip, got[:, H * W :])
    with jax.named_scope("weight_sum"):
        shares = lax.all_to_all(local, ("z", "core"), 0, 0, tiled=True)
        scale = 1.0 / math.sqrt(NZ * NY * NC * F * H * W)
        mine = (jnp.sum(shares, axis=0) * scale).astype(jnp.bfloat16)
    with jax.named_scope("gather_far"):
        far = lax.all_to_all(
            jnp.broadcast_to(mine, (16, CHUNK, CO)), TILE, 0, 0, axis_index_groups=SPARSE, tiled=True
        )
    with jax.named_scope("gather_near"):
        near = lax.all_to_all(
            jnp.broadcast_to(far, (4, 16, CHUNK, CO)), TILE, 0, 0, axis_index_groups=BLOCKS, tiled=True
        )
    with jax.named_scope("order"):
        near = near.reshape(2, 2, 2, 2, 4, 7, CJ, CO)
        half = jnp.transpose(near, (2, 5, 3, 0, 4, 1, 6, 7)).reshape(2, 7, CIN, CO)
    with jax.named_scope("swap"):
        other = lax.ppermute(half, "core", [(0, 1), (1, 0)])
        first = jnp.where(core == 0, half, other)
        second = jnp.where(core == 0, other, half)
        full = jnp.stack([first, second], axis=1).reshape(28, CIN, CO)
        weight_grad = full[:27].reshape(3, 3, 3, CIN, CO)
    with jax.named_scope("input_sum"):
        total = jnp.sum(got[:, : H * W], axis=0).astype(jnp.bfloat16)
        input_grad = jnp.transpose(total.reshape(H, W, F, CI), (2, 0, 1, 3))[None]
    return (input_grad, weight_grad)


def solution(mesh):
    grid = Mesh(mesh.devices.reshape(NZ, NY, NC, NX), AXES)
    in_specs = (
        P(TILE, None, None, None, "x"),
        P(TILE, None, None, None, "x"),
        P(None, None, None, None, "x"),
    )
    out_specs = (P(TILE, None, None, None, "x"), P(None, None, None, None, "x"))
    return jax.shard_map(shards, mesh=grid, in_specs=in_specs, out_specs=out_specs, check_vma=False)
```

time: 332 us -> 111 us (0.33)
  waiting for transfers between devices: 213 us -> 15.8 us
  blocking collectives: 13.6 us -> 68.3 us
  local copies, waits for them, and re-layouts: 50.6 us -> 4.36 us
  between operations: 16.1 us -> 0.77 us
  starting transfers between devices: 25 us -> 17.3 us
  matrix products: 4.73 us -> 0 us
  other arithmetic: 6.39 us -> 1.96 us
    psum x1 -> x0, waiting for transfers between devices: 211 us -> none  [shards(): summed = lax.psum(local, 'tile')]
    all_to_all x0 -> x4, blocking collectives: none -> 68.3 us  [the longest x1 29.6 us: shards(): shares = lax.all_to_all(local, ('z', 'core'), 0, 0, tiled=True)]
    unnamed x77 -> x3, local copies, waits for them, and re-layouts: 26.1 us -> 0.63 us
    another operation x31 -> x1, local copies, waits for them, and re-layouts: 21.2 us -> 0.19 us  [shards(): full = jnp.stack([first, second], axis=1).reshape(28, CIN, CO)]
    ppermute x8 -> x3, starting transfers between devices: 24.9 us -> 10.5 us  [the longest x1 4.81 us: shards(): north = lax.ppermute(g[:, -1:], 'z', [(i, i + 1) for i in range(NZ - 1)])]
    all_gather x1 -> x0, blocking collectives: 13.6 us -> none  [shards(): whole = lax.all_gather(activations[0], 'filt', axis=3, tiled=True)]
    all_to_all x0 -> x1, waiting for transfers between devices: none -> 11.6 us  [shards(): strip = lax.all_to_all(send, 'y', 0, 0, tiled=True)]
    all_to_all x0 -> x1, starting transfers between devices: none -> 6.82 us  [shards(): strip = lax.all_to_all(send, 'y', 0, 0, tiled=True)]
  transfers between devices with their start and end apart: 10 -> 4, of which waited for: 2 -> 3; matrix products, arithmetic and copies ran while one was open for 17% -> 1% of each run, Pallas kernels for 0% -> 0%
where the time goes in v1:
time: 111 us; the launch traced here: 110 us
  blocking collectives  68.3 us (62%)
  starting transfers between devices  17.3 us (16%)
  waiting for transfers between devices  15.8 us (14%)
  local copies, waits for them, and re-layouts  4.36 us (4%)
  other arithmetic  1.96 us (2%)
  Pallas kernels  1.5 us (1%)
    all_to_all x1, blocking collectives, shards(): shares = lax.all_to_all(local, ('z', 'core'), 0, 0, tiled=True)  29.6 us
    all_to_all x1, blocking collectives, shards(): lax.all_to_all(jnp.broadcast_to(mine, (16, CHUNK, CO)), TILE, 0, 0, axis_...  15.7 us
    all_to_all x1, blocking collectives, shards(): lax.all_to_all(jnp.broadcast_to(far, (4, 16, CHUNK, CO)), TILE, 0, 0, axi...  13.7 us
    all_to_all x1, waiting for transfers between devices, shards(): strip = lax.all_to_all(send, 'y', 0, 0, tiled=True)  11.6 us
    all_to_all x1, blocking collectives, shards(): got = lax.all_to_all(send, 'x', 0, 0, tiled=True)  9.34 us
    all_to_all x1, starting transfers between devices, shards(): strip = lax.all_to_all(send, 'y', 0, 0, tiled=True)  6.82 us
    ppermute x1, starting transfers between devices, shards(): north = lax.ppermute(g[:, -1:], 'z', [(i, i + 1) for i in range(NZ - 1)])  4.81 us
    ppermute x1, starting transfers between devices, shards(): other = lax.ppermute(half, 'core', [(0, 1), (1, 0)])  4.35 us
  transfers between devices with their start and end apart: 4, of which 3 were waited for; matrix products, arithmetic and copies ran while one was open for 1% of the time, Pallas kernels for 0%

profile of v1, /device:TPU:1, one launch (start us, length us, event | category | flops | bytes accessed | tf_op | source)
XLA Modules:
  0.0 110.0 jit_solution(14384359790841660300)
XLA Ops:
  0.6 0.0 copy-start
  0.6 0.8 fusion.4
  1.5 4.8 %collective-permute-start = (bf16[2,1,8,128]{3,2,1,0:T(8,128)(2,1)S(1)}, bf16[2,1,8,128]{3,2,1,0:T(8,128)(2,1)S(1)}, u32[]{:S(2)}, u32[]{:S(2)}) collective-permute-start(bf16[2,1,8,128]{3,2,1,0:T(8,128)(2,1)S(1)} %get-tuple-element.12), channel_id=1, source_target_pairs={{0,64},{64,128},{128,192},{192,256},{256,320},{320,384},{384,448},... | collective-permute-start | bytes 12296 | tf_op jit(solution)/shard_map/halo/ppermute | solution.py:121
  6.3 1.3 %collective-permute-start.1 = (bf16[2,1,8,128]{3,2,1,0:T(8,128)(2,1)S(1)}, bf16[2,1,8,128]{3,2,1,0:T(8,128)(2,1)S(1)}, u32[]{:S(2)}, u32[]{:S(2)}) collective-permute-start(bf16[2,1,8,128]{3,2,1,0:T(8,128)(2,1)S(1)} %get-tuple-element.13), channel_id=1, source_target_pairs={{64,0},{128,64},{192,128},{256,192},{320,256},{384,320},{448,384},... | collective-permute-start | bytes 12296 | tf_op jit(solution)/shard_map/halo/ppermute | solution.py:122
  7.6 0.8 copy.13
  8.4 0.0 collective-permute-done
  8.5 2.8 %collective-permute-done.1 = bf16[2,1,8,128]{3,2,1,0:T(8,128)(2,1)S(1)} collective-permute-done((bf16[2,1,8,128]{3,2,1,0:T(8,128)(2,1)S(1)}, bf16[2,1,8,128]{3,2,1,0:T(8,128)(2,1)S(1)}, u32[]{:S(2)}, u32[]{:S(2)}) %collective-permute-start.1) | collective-permute-done | bytes 4128 | tf_op jit(solution)/shard_map/halo/ppermute | solution.py:122
  11.3 0.8 pad_maximum_fusion.2
  12.1 0.8 fusion.1
  12.9 6.8 %all-to-all-start = ((bf16[8,176,128]{2,1,0:T(8,128)(2,1)}), bf16[8,176,128]{2,1,0:T(8,128)(2,1)S(1)}, u32[]{:S(2)}, u32[]{:S(2)}) async-start(bf16[8,176,128]{2,1,0:T(8,128)(2,1)} %fusion.1), calls=%async_computation | async-start | bytes 720896 | tf_op jit(solution)/shard_map/strip/all_to_all | solution.py:128
  19.7 11.6 %all-to-all-done.g_ref = bf16[8,176,128]{2,1,0:T(8,128)(2,1)S(1)} async-done(((bf16[8,176,128]{2,1,0:T(8,128)(2,1)}), bf16[8,176,128]{2,1,0:T(8,128)(2,1)S(1)}, u32[]{:S(2)}, u32[]{:S(2)}) %all-to-all-start) | async-done | bytes 360480 | tf_op jit(solution)/shard_map/strip/all_to_all | solution.py:128
  31.3 0.0 copy-done
  31.3 0.9 input_part.1
  32.2 9.3 %all_to_all.25 = f32[4,128,128]{2,1,0:T(8,128)S(1)} all-to-all(f32[4,128,128]{2,1,0:T(8,128)S(1)} %pad_maximum_fusion.1), channel_id=1, replica_groups=mesh['z'=8,'y'=8,'core'=2,'x'=4] {'x'}, dimensions={0} | all-to-all | bytes 524288 | tf_op jit(solution)/shard_map/filters/all_to_all | solution.py:144
  41.6 0.6 weight_part.1
  42.2 29.6 %all_to_all.26 = f32[16,56,128]{2,1,0:T(8,128)S(1)} all-to-all(f32[16,56,128]{2,1,0:T(8,128)S(1)} %weight_part.1), channel_id=1, replica_groups=mesh['z'=8,'y'=8,'core'=2,'x'=4] {'z','core'}, dimensions={0} | all-to-all | bytes 917504 | tf_op jit(solution)/shard_map/weight_sum/all_to_all | solution.py:154
  71.9 15.7 %all_to_all.27 = bf16[16,56,128]{2,1,0:T(8,128)(2,1)S(1)} all-to-all(bf16[16,56,128]{2,1,0:T(8,128)(2,1)S(1)} %broadcast_in_dim.18), channel_id=1, replica_groups={{0,16,32,48,128,144,160,176,256,272,288,304,384,400,416,432},{4,20,36,5..., dimensions={0} | all-to-all | bytes 458752 | tf_op jit(solution)/shard_map/gather_far/all_to_all | solution.py:158
  87.6 0.1 broadcast_in_dim.19
  87.7 13.7 %all_to_all.28 = bf16[4,16,56,128]{3,2,1,0:T(8,128)(2,1)S(1)} all-to-all(bf16[4,16,56,128]{3,2,1,0:T(8,128)(2,1)S(1)} %broadcast_in_dim.19), channel_id=1, replica_groups={{0,8,64,72},{4,12,68,76},{16,24,80,88},{20,28,84,92},{32,40,96,104},{36..., dimensions={0} | all-to-all | bytes 1835008 | tf_op jit(solution)/shard_map/gather_near/all_to_all | solution.py:162
  101.4 0.2 copy.14
  101.6 4.4 %collective-permute-start.2 = (bf16[2,7,256,128]{3,2,1,0:T(8,128)(2,1)S(1)}, bf16[2,7,256,128]{3,2,1,0:T(8,128)(2,1)S(1)}, u32[]{:S(2)}, u32[]{:S(2)}) collective-permute-start(bf16[2,7,256,128]{3,2,1,0:T(8,128)(2,1)S(1)} %bitcast.31), channel_id=1, source_target_pairs={{0,4},{4,0},{1,5},{5,1},{2,6},{6,2},{3,7},{7,3},{8,12},{12,8},{9,1... | collective-permute-start | bytes 2752520 | tf_op jit(solution)/shard_map/swap/ppermute | solution.py:169
  106.0 0.1 convert_element_type.21
  106.1 0.6 copy.16
  106.7 1.4 %collective-permute-done.2 = bf16[2,7,256,128]{3,2,1,0:T(8,128)(2,1)S(1)} collective-permute-done((bf16[2,7,256,128]{3,2,1,0:T(8,128)(2,1)S(1)}, bf16[2,7,256,128]{3,2,1,0:T(8,128)(2,1)S(1)}, u32[]{:S(2)}, u32[]{:S(2)}) %collective-permute-start.2) | collective-permute-done | bytes 917536 | tf_op jit(solution)/shard_map/swap/ppermute | solution.py:169
  108.1 0.2 select_bitcast_fusion.1
  108.2 0.2 pad_maximum_fusion
  108.4 0.2 copy.15
  108.6 1.3 %slice.29 = bf16[27,256,128]{2,1,0:T(8,128)(2,1)} slice(bf16[28,256,128]{2,1,0:T(8,128)(2,1)S(1)} %bitcast.29), slice={[0:27], [0:256], [0:128]} | slice | bytes 3538944 | tf_op jit(solution)/shard_map/swap/slice | solution.py:173
  (8 shorter events, 0.2 us)
Async XLA Ops:
  0.6 30.6 %copy-start = (bf16[3,3,3,256,128]{4,3,2,1,0:T(8,128)(2,1)S(1)}, bf16[3,3,3,256,128]{4,3,2,1,0:T(8,128)(2,1)}, u32[]{:S(2)}) copy-start(bf16[3,3,3,256,128]{4,3,2,1,0:T(8,128)(2,1)} %param.5) | copy-start | bytes 5308420
  1.5 7.0 %collective-permute-start = (bf16[2,1,8,128]{3,2,1,0:T(8,128)(2,1)S(1)}, bf16[2,1,8,128]{3,2,1,0:T(8,128)(2,1)S(1)}, u32[]{:S(2)}, u32[]{:S(2)}) collective-permute-start(bf16[2,1,8,128]{3,2,1,0:T(8,128)(2,1)S(1)} %get-tuple-element.12), channel_id=1, source_target_pairs={{0,64},{64,128},{128,192},{192,256},{256,320},{320,384},{384,448},... | collective-permute-start | bytes 12296 | tf_op jit(solution)/shard_map/halo/ppermute | solution.py:121
  6.3 5.0 %collective-permute-start.1 = (bf16[2,1,8,128]{3,2,1,0:T(8,128)(2,1)S(1)}, bf16[2,1,8,128]{3,2,1,0:T(8,128)(2,1)S(1)}, u32[]{:S(2)}, u32[]{:S(2)}) collective-permute-start(bf16[2,1,8,128]{3,2,1,0:T(8,128)(2,1)S(1)} %get-tuple-element.13), channel_id=1, source_target_pairs={{64,0},{128,64},{192,128},{256,192},{320,256},{384,320},{448,384},... | collective-permute-start | bytes 12296 | tf_op jit(solution)/shard_map/halo/ppermute | solution.py:122
  12.9 18.4 %all-to-all-start = ((bf16[8,176,128]{2,1,0:T(8,128)(2,1)}), bf16[8,176,128]{2,1,0:T(8,128)(2,1)S(1)}, u32[]{:S(2)}, u32[]{:S(2)}) async-start(bf16[8,176,128]{2,1,0:T(8,128)(2,1)} %fusion.1), calls=%async_computation | async-start | bytes 720896 | tf_op jit(solution)/shard_map/strip/all_to_all | solution.py:128
  101.6 6.4 %collective-permute-start.2 = (bf16[2,7,256,128]{3,2,1,0:T(8,128)(2,1)S(1)}, bf16[2,7,256,128]{3,2,1,0:T(8,128)(2,1)S(1)}, u32[]{:S(2)}, u32[]{:S(2)}) collective-permute-start(bf16[2,7,256,128]{3,2,1,0:T(8,128)(2,1)S(1)} %bitcast.31), channel_id=1, source_target_pairs={{0,4},{4,0},{1,5},{5,1},{2,6},{6,2},{3,7},{7,3},{8,12},{12,8},{9,1... | collective-permute-start | bytes 2752520 | tf_op jit(solution)/shard_map/swap/ppermute | solution.py:169

commit v2 on v1

v2 whole, which is shorter than its diff:
```python
import math

import jax
import jax.numpy as jnp
from jax import lax
from jax.experimental import pallas as pl
from jax.experimental.pallas import tpu as pltpu
from jax.sharding import Mesh
from jax.sharding import PartitionSpec as P

AXES = ("z", "y", "core", "x")
TILE = ("z", "y", "core")
NZ, NY, NC, NX = 8, 8, 2, 4
F, H, W = 2, 8, 8
CIN, COUT = 256, 512
CI, CO = CIN // NX, COUT // NX
GROWS = F * H * W
EXT = (H + 2) * W
CJ = CI // NY
XROWS = 16
TERMS = 2 * EXT
CHUNK = 7 * CJ


def tile_index(z, y, core):
    return (z * NY + y) * NC + core


SPARSE = [
    [tile_index(a + 2 * i, b + 2 * j, c) for i in range(4) for j in range(4)]
    for a in range(2)
    for b in range(2)
    for c in range(NC)
]
BLOCKS = [
    [tile_index((2 * i + pz) % NZ, (2 * j + py) % NY, c) for pz in offsets for py in offsets]
    for i in range(NZ // 2)
    for j in range(NY // 2)
    for c, offsets in enumerate(((0, 1), (2, 1)))
]


def shifted(own, left, right, tap):
    if tap == 1:
        return own
    row = lax.broadcasted_iota(jnp.int32, own.shape, own.ndim - 2)
    axis = own.ndim - 2
    if tap == 0:
        return jnp.where(row == W - 1, pltpu.roll(right, W - 1, axis), pltpu.roll(own, W - 1, axis))
    return jnp.where(row == 0, pltpu.roll(left, 1, axis), pltpu.roll(own, 1, axis))


def input_kernel(col_ref, g_ref, k_ref, out_ref):
    col = col_ref[0]

    def tile(i):
        return g_ref[i, :GROWS, :].astype(jnp.float32).reshape(F * H, W, CO)

    own = tile(col)
    left = jnp.where(col > 0, tile(jnp.maximum(col - 1, 0)), 0.0)
    right = jnp.where(col < NY - 1, tile(jnp.minimum(col + 1, NY - 1)), 0.0)
    dims = (((1,), (1,)), ((), ()))
    sums = [[jnp.zeros((H * W, CIN), jnp.float32) for _ in range(3)] for _ in range(F)]
    for te in range(3):
        rows = shifted(own, left, right, te).reshape(F, H * W, CO).astype(jnp.bfloat16)
        both = jnp.concatenate([rows[0], rows[1]], axis=1)
        for tb in range(3):
            k0, k1, k2 = (k_ref[ta * 9 + tb * 3 + te] for ta in range(3))
            for f, pair in enumerate(((k1, k0), (k2, k1))):
                sums[f][tb] += lax.dot_general(
                    both, jnp.concatenate(pair, axis=1), dims, preferred_element_type=jnp.float32
                )
    tall = []
    for f in range(F):
        total = jnp.zeros((EXT, CIN), jnp.float32)
        for tb in range(3):
            parts = [sums[f][tb]]
            if tb > 0:
                parts.insert(0, jnp.zeros((tb * W, CIN), jnp.float32))
            if tb < 2:
                parts.append(jnp.zeros(((2 - tb) * W, CIN), jnp.float32))
            total += jnp.concatenate(parts, axis=0)
        tall.append(total)
    for i in range(NX):
        cut = slice(i * CI, (i + 1) * CI)
        value = jnp.concatenate([tall[0][:, cut], tall[1][:, cut]], axis=1)
        high = value.astype(jnp.bfloat16)
        out_ref[i, :EXT, :] = high
        out_ref[i, EXT:, :] = (value - high.astype(jnp.float32)).astype(jnp.bfloat16)


def weight_kernel(place_ref, own_ref, pair_ref, north_ref, south_ref, got_ref, out_ref, inner_ref, acc_ref):
    core, row = place_ref[0], place_ref[1]
    terms = got_ref[:, :TERMS, :].astype(jnp.float32)
    terms = terms[:, :EXT, :] + terms[:, EXT:, :]
    terms = (terms[0] + terms[1]) + (terms[2] + terms[3])
    inner_ref[...] = terms[W : EXT - W]
    for z in range(NZ):
        up = jnp.where(row - 1 == z, terms[:W], 0.0)
        out_ref[z, CHUNK:, :] = jnp.where(row + 1 == z, terms[EXT - W :], up)

    x = got_ref[:, TERMS:, :].astype(jnp.float32).reshape(NX, NC, NY, CJ, F * H * W)
    frames = []
    for f in range(F):
        cut = slice(f * H * W, (f + 1) * H * W)
        cols = [
            x[:, clip, y, :, cut].reshape(NX * CJ, H * W) for clip in range(NC) for y in range(NY)
        ]
        frames.append(jnp.concatenate(cols, axis=1))
    xs = jnp.concatenate(frames, axis=0).astype(jnp.bfloat16)
    half = NX * CJ
    talls = []
    for clip, ref in enumerate((own_ref, pair_ref)):
        rows = ref[:, :GROWS, :].astype(jnp.float32).reshape(NY, F, H, W, CO)
        north = north_ref[clip].astype(jnp.float32).reshape(NY, F, 1, W, CO)
        south = south_ref[clip].astype(jnp.float32).reshape(NY, F, 1, W, CO)
        talls.append(jnp.concatenate([north, rows, south], axis=2).reshape(NY, F * (H + 2), W, CO))
    edge = jnp.zeros((1, F * (H + 2), W, CO), jnp.float32)
    for te in range(3):
        moved = []
        for tall in talls:
            left = jnp.concatenate([edge, tall[:-1]], axis=0)
            right = jnp.concatenate([tall[1:], edge], axis=0)
            moved.append(shifted(tall, left, right, te).reshape(NY, F, H + 2, W, CO))
        for tb in range(3):
            cols = []
            for f in range(F):
                rows = [m[:, f, 2 - tb : 2 - tb + H].reshape(NY * H * W, CO) for m in moved]
                cols.append(jnp.concatenate(rows, axis=0).astype(jnp.bfloat16))
            both = jnp.concatenate(cols, axis=1)
            prod = jnp.dot(xs, both, preferred_element_type=jnp.float32)
            parts = (
                prod[:half, CO:],
                prod[:half, :CO] + prod[half:, CO:],
                prod[half:, :CO],
            )
            for ta in range(3):
                group, t = divmod(ta * 9 + tb * 3 + te, 7)
                for q in range(NX):
                    acc_ref[group % 2, (group // 2) * NX + q, t * CJ : (t + 1) * CJ, :] = parts[ta][
                        q * CJ : (q + 1) * CJ
                    ]
    for q in range(NX):
        acc_ref[1, NX + q, 6 * CJ :, :] = jnp.zeros((CJ, CO), jnp.float32)
    out_ref[:, :CHUNK, :] = acc_ref[core]


def shards(activations, out_grad, kernel):
    col = lax.axis_index("y").astype(jnp.int32)
    core = lax.axis_index("core").astype(jnp.int32)
    row = lax.axis_index("z").astype(jnp.int32)
    smem = pl.BlockSpec(memory_space=pltpu.SMEM)
    vmem = pl.BlockSpec(memory_space=pltpu.VMEM)
    params = pltpu.CompilerParams(vmem_limit_bytes=32 * 1024 * 1024)
    swap = [(0, 1), (1, 0)]
    with jax.named_scope("strip"):
        xt = activations[0].reshape(F * H * W, CI).T.reshape(NY, CJ, F * H * W)
        xt = jnp.pad(xt, ((0, 0), (0, XROWS - CJ), (0, 0)))
        rows = jnp.broadcast_to(out_grad[0].reshape(GROWS, CO), (NY, GROWS, CO))
        strip = lax.all_to_all(jnp.concatenate([rows, xt], axis=1), "y", 0, 0, tiled=True)
    with jax.named_scope("clips"):
        pair = lax.ppermute(strip, "core", swap)
    with jax.named_scope("input_part"):
        terms = pl.pallas_call(
            input_kernel,
            out_shape=jax.ShapeDtypeStruct((NX, TERMS, F * CI), jnp.bfloat16),
            in_specs=[smem, vmem, vmem],
            out_specs=vmem,
            compiler_params=params,
        )(col.reshape(1), strip, kernel.reshape(27, CIN, CO))
    with jax.named_scope("edges"):
        both = jnp.stack([strip[:, :GROWS], pair[:, :GROWS]]).reshape(NC, NY, F, H, W, CO)
        north = lax.ppermute(both[:, :, :, H - 1], "z", [(i, i + 1) for i in range(NZ - 1)])
        south = lax.ppermute(both[:, :, :, 0], "z", [(i + 1, i) for i in range(NZ - 1)])
    with jax.named_scope("filters"):
        xmine = [s[:, GROWS : GROWS + CJ].reshape(NY * CJ, F * H * W) for s in (strip, pair)]
        xmine = jnp.broadcast_to(jnp.concatenate(xmine, axis=0), (NX, NC * NY * CJ, F * H * W))
        got = lax.all_to_all(jnp.concatenate([terms, xmine], axis=1), "x", 0, 0, tiled=True)
    with jax.named_scope("weight_part"):
        local, inner = pl.pallas_call(
            weight_kernel,
            out_shape=[
                jax.ShapeDtypeStruct((NZ, CHUNK + W, CO), jnp.float32),
                jax.ShapeDtypeStruct((H * W, F * CI), jnp.float32),
            ],
            in_specs=[smem] + [vmem] * 5,
            out_specs=[vmem] * 2,
            scratch_shapes=[pltpu.VMEM((NC, NZ, CHUNK, CO), jnp.float32)],
            compiler_params=params,
        )(jnp.stack([core, row]), strip, pair, north, south, got)
    with jax.named_scope("weight_sum"):
        shares = lax.all_to_all(local, "z", 0, 0, tiled=True)
        scale = 1.0 / math.sqrt(NZ * NY * NC * F * H * W)
        mine = (jnp.sum(shares[:, :CHUNK], axis=0) * scale).astype(jnp.bfloat16)
    with jax.named_scope("gather_far"):
        far = lax.all_to_all(
            jnp.broadcast_to(mine, (16, CHUNK, CO)), TILE, 0, 0, axis_index_groups=SPARSE, tiled=True
        )
    with jax.named_scope("gather_near"):
        near = lax.all_to_all(
            jnp.broadcast_to(far, (4, 16, CHUNK, CO)), TILE, 0, 0, axis_index_groups=BLOCKS, tiled=True
        )
    with jax.named_scope("order"):
        near = near.reshape(2, 2, 2, 2, 4, 7, CJ, CO)
        half = jnp.transpose(near, (2, 5, 3, 0, 4, 1, 6, 7)).reshape(2, 7, CIN, CO)
    with jax.named_scope("swap"):
        other = lax.ppermute(half, "core", swap)
        first = jnp.where(core == 0, half, other)
        second = jnp.where(core == 0, other, half)
        full = jnp.concatenate([first[0], second[0], first[1], second[1, :6]], axis=0)
        weight_grad = full.reshape(3, 3, 3, CIN, CO)
    with jax.named_scope("input_sum"):
        source = lax.broadcasted_iota(jnp.int32, (NZ, W, F * CI), 0)
        edges = shares[:, CHUNK:]
        above = jnp.sum(jnp.where(source < row, edges, 0.0), axis=0)
        below = jnp.sum(jnp.where(source > row, edges, 0.0), axis=0)
        total = inner.reshape(H, W, F * CI)
        total = jnp.concatenate([total[:1] + above, total[1:-1], total[-1:] + below], axis=0)
        total = total.astype(jnp.bfloat16).reshape(H, W, F, CI)
        input_grad = jnp.transpose(total, (2, 0, 1, 3))[None]
    return (input_grad, weight_grad)


def solution(mesh):
    grid = Mesh(mesh.devices.reshape(NZ, NY, NC, NX), AXES)
    in_specs = (
        P(TILE, None, None, None, "x"),
        P(TILE, None, None, None, "x"),
        P(None, None, None, None, "x"),
    )
    out_specs = (P(TILE, None, None, None, "x"), P(None, None, None, None, "x"))
    return jax.shard_map(shards, mesh=grid, in_specs=in_specs, out_specs=out_specs, check_vma=False)
```

time: 111 us -> 97.5 us (0.88)
  waiting for transfers between devices: 15.8 us -> 2.48 us
  blocking collectives: 68.3 us -> 65.4 us
  starting transfers between devices: 17.3 us -> 19.9 us
  local copies, waits for them, and re-layouts: 4.36 us -> 2.65 us
  other arithmetic: 1.96 us -> 3.24 us
    all_to_all x1, waiting for transfers between devices: 11.6 us -> 0.01 us  [shards(): lax.all_to_all(jnp.concatenate([terms, xmine], axis=1), 'x', 0, 0, tiled=...]
    ppermute x3 -> x4, starting transfers between devices: 10.5 us -> 15.9 us  [the longest x1 5.25 us: shards(): pair = lax.ppermute(strip, 'core', swap)]
    all_to_all x1, starting transfers between devices: 6.82 us -> 4.01 us  [shards(): lax.all_to_all(jnp.concatenate([terms, xmine], axis=1), 'x', 0, 0, tiled=...]
    slice x2 -> x3, local copies, waits for them, and re-layouts: 2.17 us -> 0.04 us  [the longest x1 0.02 us: shards(): strip[:, :GROWS]]
    ppermute x3 -> x4, waiting for transfers between devices: 4.2 us -> 2.47 us  [the longest x1 1.23 us: shards(): lax.ppermute(both[:, :, :, H - 1], 'z', [(i, i + 1) for i in range(NZ - 1)])]
    all_to_all x2, blocking collectives: 39 us -> 37.6 us  [the longest x1 19.9 us: shards(): shares = lax.all_to_all(local, 'z', 0, 0, tiled=True)]
    all_to_all x1, blocking collectives: 15.7 us -> 14.5 us  [shards(): lax.all_to_all(jnp.broadcast_to(mine, (16, CHUNK, CO)), TILE, 0, 0, axis_...]
  transfers between devices with their start and end apart: 4 -> 5, of which waited for: 3 -> 3; matrix products, arithmetic and copies ran while one was open for 1% -> 1% of each run, Pallas kernels for 0% -> 1%
where the time goes in v2:
time: 97.5 us; the launch traced here: 97 us
  blocking collectives  65.4 us (67%)
  starting transfers between devices  19.9 us (20%)
  other arithmetic  3.24 us (3%)
  local copies, waits for them, and re-layouts  2.65 us (3%)
  Pallas kernels  2.55 us (3%)
  waiting for transfers between devices  2.48 us (3%)
    all_to_all x1, blocking collectives, shards(): shares = lax.all_to_all(local, 'z', 0, 0, tiled=True)  19.9 us
    all_to_all x1, blocking collectives, shards(): lax.all_to_all(jnp.concatenate([rows, xt], axis=1), 'y', 0, 0, tiled=True)  17.6 us
    all_to_all x1, blocking collectives, shards(): lax.all_to_all(jnp.broadcast_to(mine, (16, CHUNK, CO)), TILE, 0, 0, axis_...  14.5 us
    all_to_all x1, blocking collectives, shards(): lax.all_to_all(jnp.broadcast_to(far, (4, 16, CHUNK, CO)), TILE, 0, 0, axi...  13.3 us
    ppermute x1, starting transfers between devices, shards(): pair = lax.ppermute(strip, 'core', swap)  5.25 us
    ppermute x1, starting transfers between devices, shards(): other = lax.ppermute(half, 'core', swap)  4.74 us
    ppermute x1, starting transfers between devices, shards(): lax.ppermute(both[:, :, :, H - 1], 'z', [(i, i + 1) for i in range(NZ - 1)])  4.63 us
    all_to_all x1, starting transfers between devices, shards(): lax.all_to_all(jnp.concatenate([terms, xmine], axis=1), 'x', 0, 0, tiled=...  4.01 us
  transfers between devices with their start and end apart: 5, of which 3 were waited for; matrix products, arithmetic and copies ran while one was open for 1% of the time, Pallas kernels for 1%

profile of v2, /device:TPU:1, one launch (start us, length us, event | category | flops | bytes accessed | tf_op | source)
XLA Modules:
  0.0 97.0 jit_solution(2090475785459228524)
XLA Ops:
  0.6 0.0 copy-start
  0.6 1.0 copy.15
  1.6 0.8 broadcast_in_dim.22
  2.4 17.6 %all_to_all.25.g_ref.own_ref = bf16[8,144,128]{2,1,0:T(8,128)(2,1)S(1)} all-to-all(bf16[8,144,128]{2,1,0:T(8,128)(2,1)S(1)} %fusion.1), channel_id=1, replica_groups=mesh['z'=8,'y'=8,'core'=2,'x'=4] {'y'}, dimensions={0} | all-to-all | bytes 589824 | tf_op jit(solution)/shard_map/strip/all_to_all | solution.py:160
  20.1 5.2 %collective-permute-start = (bf16[8,144,128]{2,1,0:T(8,128)(2,1)S(1)}, bf16[8,144,128]{2,1,0:T(8,128)(2,1)S(1)}, u32[]{:S(2)}, u32[]{:S(2)}) collective-permute-start(bf16[8,144,128]{2,1,0:T(8,128)(2,1)S(1)} %all_to_all.25.g_ref.own_ref), channel_id=1, source_target_pairs={{0,4},{4,0},{1,5},{5,1},{2,6},{6,2},{3,7},{7,3},{8,12},{12,8},{9,1... | collective-permute-start | bytes 884744 | tf_op jit(solution)/shard_map/clips/ppermute | solution.py:162
  25.4 0.0 copy-done
  25.4 0.9 input_part.1
  26.3 0.2 collective-permute-done.pair_ref
  26.6 0.7 pad_maximum_fusion.1
  27.3 4.0 %all-to-all-start.1 = ((bf16[4,288,128]{2,1,0:T(8,128)(2,1)}), bf16[4,288,128]{2,1,0:T(8,128)(2,1)S(1)}, u32[]{:S(2)}, u32[]{:S(2)}) async-start(bf16[4,288,128]{2,1,0:T(8,128)(2,1)} %pad_maximum_fusion.1), calls=%async_computation.1 | async-start | bytes 589824 | tf_op jit(solution)/shard_map/filters/all_to_all | solution.py:178
  31.4 1.3 %collective-permute-start.2 = (bf16[2,8,2,8,128]{4,3,2,1,0:T(8,128)(2,1)S(1)}, bf16[2,8,2,8,128]{4,3,2,1,0:T(8,128)(2,1)S(1)}, u32[]{:S(2)}, u32[]{:S(2)}) collective-permute-start(bf16[2,8,2,8,128]{4,3,2,1,0:T(8,128)(2,1)S(1)} %get-tuple-element.12), channel_id=1, source_target_pairs={{64,0},{128,64},{192,128},{256,192},{320,256},{384,320},{448,384},... | collective-permute-start | bytes 196616 | tf_op jit(solution)/shard_map/edges/ppermute | solution.py:174
  32.7 4.6 %collective-permute-start.1 = (bf16[2,8,2,8,128]{4,3,2,1,0:T(8,128)(2,1)S(1)}, bf16[2,8,2,8,128]{4,3,2,1,0:T(8,128)(2,1)S(1)}, u32[]{:S(2)}, u32[]{:S(2)}) collective-permute-start(bf16[2,8,2,8,128]{4,3,2,1,0:T(8,128)(2,1)S(1)} %get-tuple-element.13), channel_id=1, source_target_pairs={{0,64},{64,128},{128,192},{192,256},{256,320},{320,384},{384,448},... | collective-permute-start | bytes 196616 | tf_op jit(solution)/shard_map/edges/ppermute | solution.py:173
  37.3 0.1 pad_add_fusion.place_ref
  37.4 0.0 collective-permute-done.2.south_ref
  37.4 1.2 %collective-permute-done.1.north_ref = bf16[2,8,2,8,128]{4,3,2,1,0:T(8,128)(2,1)S(1)} collective-permute-done((bf16[2,8,2,8,128]{4,3,2,1,0:T(8,128)(2,1)S(1)}, bf16[2,8,2,8,128]{4,3,2,1,0:T(8,128)(2,1)S(1)}, u32[]{:S(2)}, u32[]{:S(2)}) %collective-permute-start.1) | collective-permute-done | bytes 65568 | tf_op jit(solution)/shard_map/edges/ppermute | solution.py:173
  38.6 0.0 all-to-all-done.1.got_ref
  38.6 1.6 %weight_part.1 = (f32[8,64,128]{2,1,0:T(8,128)S(1)}, f32[64,128]{1,0:T(8,128)S(1)}) custom-call(s32[2]{0:T(128)S(1)} %pad_add_fusion.place_ref, bf16[8,144,128]{2,1,0:T(8,128)(2,1)S(1)} %all_to_all.25.g_ref.own_ref, bf16[8,144,128]{2,1,0:T(8,128)(2,1)S(1)} %collective-permute-done.pair_ref, bf16[2,8,2,8,128]{4,3,2,1,0:T(8,128)(2,1)S(1)} %collective-permute-done.1.north_ref, ...), custom_call_target="tpu_custom_call" | custom-call | tf_op jit(solution)/shard_map/weight_part/pallas_call | solution.py:180
  40.2 19.9 %all_to_all.26 = f32[8,64,128]{2,1,0:T(8,128)S(1)} all-to-all(f32[8,64,128]{2,1,0:T(8,128)S(1)} %get-tuple-element.5), channel_id=1, replica_groups=mesh['z'=8,'y'=8,'core'=2,'x'=4] {'z'}, dimensions={0} | all-to-all | bytes 524288 | tf_op jit(solution)/shard_map/weight_sum/all_to_all | solution.py:192
  60.2 14.5 %all_to_all.27 = bf16[16,56,128]{2,1,0:T(8,128)(2,1)S(1)} all-to-all(bf16[16,56,128]{2,1,0:T(8,128)(2,1)S(1)} %broadcast_in_dim.26), channel_id=1, replica_groups={{0,16,32,48,128,144,160,176,256,272,288,304,384,400,416,432},{4,20,36,5..., dimensions={0} | all-to-all | bytes 458752 | tf_op jit(solution)/shard_map/gather_far/all_to_all | solution.py:196
  74.7 0.1 broadcast_in_dim.27
  74.8 13.3 %all_to_all.28 = bf16[4,16,56,128]{3,2,1,0:T(8,128)(2,1)S(1)} all-to-all(bf16[4,16,56,128]{3,2,1,0:T(8,128)(2,1)S(1)} %broadcast_in_dim.27), channel_id=1, replica_groups={{0,8,64,72},{148,140,84,76},{16,24,80,88},{164,156,100,92},{32,40,96,10..., dimensions={0} | all-to-all | bytes 1835008 | tf_op jit(solution)/shard_map/gather_near/all_to_all | solution.py:200
  88.2 0.2 copy.21
  88.4 4.7 %collective-permute-start.3 = (bf16[2,7,256,128]{3,2,1,0:T(8,128)(2,1)S(1)}, bf16[2,7,256,128]{3,2,1,0:T(8,128)(2,1)S(1)}, u32[]{:S(2)}, u32[]{:S(2)}) collective-permute-start(bf16[2,7,256,128]{3,2,1,0:T(8,128)(2,1)S(1)} %bitcast.44), channel_id=1, source_target_pairs={{0,4},{4,0},{1,5},{5,1},{2,6},{6,2},{3,7},{7,3},{8,12},{12,8},{9,1... | collective-permute-start | bytes 2752520 | tf_op jit(solution)/shard_map/swap/ppermute | solution.py:207
  93.2 0.1 concatenate.28
  93.3 0.1 select_reduce_fusion.1
  93.4 0.1 concatenate.27
  93.5 0.1 concatenate.29
  93.6 0.6 maximum_bitcast_fusion.1
  94.2 1.0 %collective-permute-done.3 = bf16[2,7,256,128]{3,2,1,0:T(8,128)(2,1)S(1)} collective-permute-done((bf16[2,7,256,128]{3,2,1,0:T(8,128)(2,1)S(1)}, bf16[2,7,256,128]{3,2,1,0:T(8,128)(2,1)S(1)}, u32[]{:S(2)}, u32[]{:S(2)}) %collective-permute-start.3) | collective-permute-done | bytes 917536 | tf_op jit(solution)/shard_map/swap/ppermute | solution.py:207
  95.3 0.2 broadcast_select_fusion.1
  95.5 0.1 slice_bitcast_fusion.2
  95.6 1.4 %pad_maximum_fusion = bf16[27,256,128]{2,1,0:T(8,128)(2,1)} fusion(bf16[6,256,128]{2,1,0:T(8,128)(2,1)S(1)} %slice_bitcast_fusion.3, bf16[7,256,128]{2,1,0:T(8,128)(2,1)S(1)} %get-tuple-element.11, bf16[7,256,128]{2,1,0:T(8,128)(2,1)S(1)} %get-tuple-element.18, bf16[7,256,128]{2,1,0:T(8,128)(2,1)S(1)} %get-tuple-element.10), kind=kLoop, calls=%fused_computation | loop fusion | flops 2654208 | bytes 3538944 | tf_op jit(solution)/shard_map/swap/concatenate | solution.py:210
  (18 shorter events, 0.2 us)
Async XLA Ops:
  0.6 24.7 %copy-start = (bf16[3,3,3,256,128]{4,3,2,1,0:T(8,128)(2,1)S(1)}, bf16[3,3,3,256,128]{4,3,2,1,0:T(8,128)(2,1)}, u32[]{:S(2)}) copy-start(bf16[3,3,3,256,128]{4,3,2,1,0:T(8,128)(2,1)} %param.5) | copy-start | bytes 5308420
  20.1 6.4 %collective-permute-start = (bf16[8,144,128]{2,1,0:T(8,128)(2,1)S(1)}, bf16[8,144,128]{2,1,0:T(8,128)(2,1)S(1)}, u32[]{:S(2)}, u32[]{:S(2)}) collective-permute-start(bf16[8,144,128]{2,1,0:T(8,128)(2,1)S(1)} %all_to_all.25.g_ref.own_ref), channel_id=1, source_target_pairs={{0,4},{4,0},{1,5},{5,1},{2,6},{6,2},{3,7},{7,3},{8,12},{12,8},{9,1... | collective-permute-start | bytes 884744 | tf_op jit(solution)/shard_map/clips/ppermute | solution.py:162
  27.3 11.3 %all-to-all-start.1 = ((bf16[4,288,128]{2,1,0:T(8,128)(2,1)}), bf16[4,288,128]{2,1,0:T(8,128)(2,1)S(1)}, u32[]{:S(2)}, u32[]{:S(2)}) async-start(bf16[4,288,128]{2,1,0:T(8,128)(2,1)} %pad_maximum_fusion.1), calls=%async_computation.1 | async-start | bytes 589824 | tf_op jit(solution)/shard_map/filters/all_to_all | solution.py:178
  31.4 6.0 %collective-permute-start.2 = (bf16[2,8,2,8,128]{4,3,2,1,0:T(8,128)(2,1)S(1)}, bf16[2,8,2,8,128]{4,3,2,1,0:T(8,128)(2,1)S(1)}, u32[]{:S(2)}, u32[]{:S(2)}) collective-permute-start(bf16[2,8,2,8,128]{4,3,2,1,0:T(8,128)(2,1)S(1)} %get-tuple-element.12), channel_id=1, source_target_pairs={{64,0},{128,64},{192,128},{256,192},{320,256},{384,320},{448,384},... | collective-permute-start | bytes 196616 | tf_op jit(solution)/shard_map/edges/ppermute | solution.py:174
  32.7 5.9 %collective-permute-start.1 = (bf16[2,8,2,8,128]{4,3,2,1,0:T(8,128)(2,1)S(1)}, bf16[2,8,2,8,128]{4,3,2,1,0:T(8,128)(2,1)S(1)}, u32[]{:S(2)}, u32[]{:S(2)}) collective-permute-start(bf16[2,8,2,8,128]{4,3,2,1,0:T(8,128)(2,1)S(1)} %get-tuple-element.13), channel_id=1, source_target_pairs={{0,64},{64,128},{128,192},{192,256},{256,320},{320,384},{384,448},... | collective-permute-start | bytes 196616 | tf_op jit(solution)/shard_map/edges/ppermute | solution.py:173
  88.4 6.8 %collective-permute-start.3 = (bf16[2,7,256,128]{3,2,1,0:T(8,128)(2,1)S(1)}, bf16[2,7,256,128]{3,2,1,0:T(8,128)(2,1)S(1)}, u32[]{:S(2)}, u32[]{:S(2)}) collective-permute-start(bf16[2,7,256,128]{3,2,1,0:T(8,128)(2,1)S(1)} %bitcast.44), channel_id=1, source_target_pairs={{0,4},{4,0},{1,5},{5,1},{2,6},{6,2},{3,7},{7,3},{8,12},{12,8},{9,1... | collective-permute-start | bytes 2752520 | tf_op jit(solution)/shard_map/swap/ppermute | solution.py:207

commit v3 on v2

--- a/solution.py
+++ b/solution.py
@@ -89,7 +89,7 @@
         out_ref[i, EXT:, :] = (value - high.astype(jnp.float32)).astype(jnp.bfloat16)
 
 
-def weight_kernel(place_ref, own_ref, pair_ref, north_ref, south_ref, got_ref, out_ref, inner_ref, acc_ref):
+def weight_kernel(place_ref, own_ref, pair_ref, edge_ref, got_ref, out_ref, inner_ref, mid_ref):
     core, row = place_ref[0], place_ref[1]
     terms = got_ref[:, :TERMS, :].astype(jnp.float32)
     terms = terms[:, :EXT, :] + terms[:, EXT:, :]
@@ -109,40 +109,41 @@
         frames.append(jnp.concatenate(cols, axis=1))
     xs = jnp.concatenate(frames, axis=0).astype(jnp.bfloat16)
     half = NX * CJ
-    talls = []
+    mids, sides = [], []
     for clip, ref in enumerate((own_ref, pair_ref)):
         rows = ref[:, :GROWS, :].astype(jnp.float32).reshape(NY, F, H, W, CO)
-        north = north_ref[clip].astype(jnp.float32).reshape(NY, F, 1, W, CO)
-        south = south_ref[clip].astype(jnp.float32).reshape(NY, F, 1, W, CO)
-        talls.append(jnp.concatenate([north, rows, south], axis=2).reshape(NY, F * (H + 2), W, CO))
-    edge = jnp.zeros((1, F * (H + 2), W, CO), jnp.float32)
+        edge = edge_ref[clip].astype(jnp.float32).reshape(NY, F, 1, W, CO)
+        below = jnp.concatenate([rows[:, :, 1:], edge], axis=2)
+        above = jnp.concatenate([edge, rows[:, :, :-1]], axis=2)
+        mids.append(rows.reshape(NY, F * H, W, CO))
+        sides.append(jnp.where(core == 0, below, above).reshape(NY, F * H, W, CO))
+    border = jnp.zeros((1, F * H, W, CO), jnp.float32)
+
+    def product(clips, te):
+        cols = [[], []]
+        for rows in clips:
+            left = jnp.concatenate([border, rows[:-1]], axis=0)
+            right = jnp.concatenate([rows[1:], border], axis=0)
+            moved = shifted(rows, left, right, te).reshape(NY, F, H * W, CO)
+            for f in range(F):
+                cols[f].append(moved[:, f].reshape(NY * H * W, CO))
+        both = [jnp.concatenate(c, axis=0).astype(jnp.bfloat16) for c in cols]
+        prod = jnp.dot(xs, jnp.concatenate(both, axis=1), preferred_element_type=jnp.float32)
+        return prod[:half, CO:], prod[:half, :CO] + prod[half:, CO:], prod[half:, :CO]
+
+    def put(slot, value):
+        group, t = divmod(slot, 7)
+        for q in range(NX):
+            out_ref[group * NX + q, t * CJ : (t + 1) * CJ, :] = value[q * CJ : (q + 1) * CJ]
+
     for te in range(3):
-        moved = []
-        for tall in talls:
-            left = jnp.concatenate([edge, tall[:-1]], axis=0)
-            right = jnp.concatenate([tall[1:], edge], axis=0)
-            moved.append(shifted(tall, left, right, te).reshape(NY, F, H + 2, W, CO))
-        for tb in range(3):
-            cols = []
-            for f in range(F):
-                rows = [m[:, f, 2 - tb : 2 - tb + H].reshape(NY * H * W, CO) for m in moved]
-                cols.append(jnp.concatenate(rows, axis=0).astype(jnp.bfloat16))
-            both = jnp.concatenate(cols, axis=1)
-            prod = jnp.dot(xs, both, preferred_element_type=jnp.float32)
-            parts = (
-                prod[:half, CO:],
-                prod[:half, :CO] + prod[half:, CO:],
-                prod[half:, :CO],
-            )
-            for ta in range(3):
-                group, t = divmod(ta * 9 + tb * 3 + te, 7)
-                for q in range(NX):
-                    acc_ref[group % 2, (group // 2) * NX + q, t * CJ : (t + 1) * CJ, :] = parts[ta][
-                        q * CJ : (q + 1) * CJ
-                    ]
-    for q in range(NX):
-        acc_ref[1, NX + q, 6 * CJ :, :] = jnp.zeros((CJ, CO), jnp.float32)
-    out_ref[:, :CHUNK, :] = acc_ref[core]
+        for ta, value in enumerate(product(sides, te)):
+            put(ta * 3 + te, value)
+        for ta, value in enumerate(product(mids, te)):
+            mid_ref[ta * 3 + te] = value
+    mid_ref[9] = jnp.zeros((half, CO), jnp.float32)
+    for i in range(5):
+        put(9 + i, mid_ref[i + 5 * core])
 
 
 def shards(activations, out_grad, kernel):
@@ -170,8 +171,10 @@
         )(col.reshape(1), strip, kernel.reshape(27, CIN, CO))
     with jax.named_scope("edges"):
         both = jnp.stack([strip[:, :GROWS], pair[:, :GROWS]]).reshape(NC, NY, F, H, W, CO)
-        north = lax.ppermute(both[:, :, :, H - 1], "z", [(i, i + 1) for i in range(NZ - 1)])
-        south = lax.ppermute(both[:, :, :, 0], "z", [(i + 1, i) for i in range(NZ - 1)])
+        edge = jnp.where(core == 0, both[:, :, :, 0], both[:, :, :, H - 1])
+        route = [(z * NC, (z - 1) * NC) for z in range(1, NZ)]
+        route += [(z * NC + 1, (z + 1) * NC + 1) for z in range(NZ - 1)]
+        edge = lax.ppermute(edge, ("z", "core"), route)
     with jax.named_scope("filters"):
         xmine = [s[:, GROWS : GROWS + CJ].reshape(NY * CJ, F * H * W) for s in (strip, pair)]
         xmine = jnp.broadcast_to(jnp.concatenate(xmine, axis=0), (NX, NC * NY * CJ, F * H * W))
@@ -183,11 +186,11 @@
                 jax.ShapeDtypeStruct((NZ, CHUNK + W, CO), jnp.float32),
                 jax.ShapeDtypeStruct((H * W, F * CI), jnp.float32),
             ],
-            in_specs=[smem] + [vmem] * 5,
+            in_specs=[smem] + [vmem] * 4,
             out_specs=[vmem] * 2,
-            scratch_shapes=[pltpu.VMEM((NC, NZ, CHUNK, CO), jnp.float32)],
+            scratch_shapes=[pltpu.VMEM((10, NX * CJ, CO), jnp.float32)],
             compiler_params=params,
-        )(jnp.stack([core, row]), strip, pair, north, south, got)
+        )(jnp.stack([core, row]), strip, pair, edge, got)
     with jax.named_scope("weight_sum"):
         shares = lax.all_to_all(local, "z", 0, 0, tiled=True)
         scale = 1.0 / math.sqrt(NZ * NY * NC * F * H * W)
@@ -202,12 +205,17 @@
         )
     with jax.named_scope("order"):
         near = near.reshape(2, 2, 2, 2, 4, 7, CJ, CO)
-        half = jnp.transpose(near, (2, 5, 3, 0, 4, 1, 6, 7)).reshape(2, 7, CIN, CO)
+        half = jnp.transpose(near, (2, 5, 3, 0, 4, 1, 6, 7)).reshape(14, CIN, CO)
     with jax.named_scope("swap"):
         other = lax.ppermute(half, "core", swap)
         first = jnp.where(core == 0, half, other)
         second = jnp.where(core == 0, other, half)
-        full = jnp.concatenate([first[0], second[0], first[1], second[1, :6]], axis=0)
+        order = [
+            (first[0:3], first[9:12], second[0:3]),
+            (first[3:6], first[12:14], second[9:10], second[3:6]),
+            (first[6:9], second[10:13], second[6:9]),
+        ]
+        full = jnp.concatenate([piece for row_taps in order for piece in row_taps], axis=0)
         weight_grad = full.reshape(3, 3, 3, CIN, CO)
     with jax.named_scope("input_sum"):
         source = lax.broadcasted_iota(jnp.int32, (NZ, W, F * CI), 0)

time: 97.5 us -> 95.8 us (0.983)
  starting transfers between devices: 19.9 us -> 17.5 us
  other arithmetic: 3.24 us -> 1.74 us
  local copies, waits for them, and re-layouts: 2.65 us -> 3.94 us
    ppermute x2 -> x1, starting transfers between devices: 5.92 us -> 4 us  [shards(): edge = lax.ppermute(edge, ('z', 'core'), route)]
    concatenate x1 -> x0, other arithmetic: 1.44 us -> none  [shards(): jnp.concatenate([first[0], second[0], first[1], second[1, :6]], axis=0)]
    unnamed x2 -> x13, local copies, waits for them, and re-layouts: 0.01 us -> 1.42 us
  transfers between devices with their start and end apart: 5 -> 4, of which waited for: 3 -> 4; matrix products, arithmetic and copies ran while one was open for 1% -> 1% of each run, Pallas kernels for 1% -> 1%
where the time goes in v3:
time: 95.8 us; the launch traced here: 95.4 us
  blocking collectives  65.6 us (68%)
  starting transfers between devices  17.5 us (18%)
  local copies, waits for them, and re-layouts  3.94 us (4%)
  waiting for transfers between devices  3.26 us (3%)
  Pallas kernels  2.47 us (3%)
  other arithmetic  1.74 us (2%)
    all_to_all x1, blocking collectives, shards(): shares = lax.all_to_all(local, 'z', 0, 0, tiled=True)  19.9 us
    all_to_all x1, blocking collectives, shards(): lax.all_to_all(jnp.concatenate([rows, xt], axis=1), 'y', 0, 0, tiled=True)  17.6 us
    all_to_all x1, blocking collectives, shards(): lax.all_to_all(jnp.broadcast_to(mine, (16, CHUNK, CO)), TILE, 0, 0, axis_...  14.7 us
    all_to_all x1, blocking collectives, shards(): lax.all_to_all(jnp.broadcast_to(far, (4, 16, CHUNK, CO)), TILE, 0, 0, axi...  13.3 us
    ppermute x1, starting transfers between devices, shards(): pair = lax.ppermute(strip, 'core', swap)  5.25 us
    ppermute x1, starting transfers between devices, shards(): other = lax.ppermute(half, 'core', swap)  4.25 us
    all_to_all x1, starting transfers between devices, shards(): lax.all_to_all(jnp.concatenate([terms, xmine], axis=1), 'x', 0, 0, tiled=...  4.01 us
    ppermute x1, starting transfers between devices, shards(): edge = lax.ppermute(edge, ('z', 'core'), route)  4 us
  transfers between devices with their start and end apart: 4, of which 4 were waited for; matrix products, arithmetic and copies ran while one was open for 1% of the time, Pallas kernels for 1%

profile of v3, /device:TPU:1, one launch (start us, length us, event | category | flops | bytes accessed | tf_op | source)
XLA Modules:
  0.0 95.4 jit_solution(817407928270098703)
XLA Ops:
  0.6 0.0 copy-start
  0.6 1.0 %copy.15 = bf16[128,64]{0,1:T(8,128)(2,1)S(1)} copy(bf16[128,64]{1,0:T(8,128)(2,1)} %bitcast.44) | data formatting | bytes 32768 | tf_op jit(solution)/shard_map/strip/reshape;strip/squeeze | solution.py:158
  1.6 0.8 broadcast_in_dim.22
  2.4 17.6 %all_to_all.25.g_ref.own_ref = bf16[8,144,128]{2,1,0:T(8,128)(2,1)S(1)} all-to-all(bf16[8,144,128]{2,1,0:T(8,128)(2,1)S(1)} %fusion.1), channel_id=1, replica_groups=mesh['z'=8,'y'=8,'core'=2,'x'=4] {'y'}, dimensions={0} | all-to-all | bytes 589824 | tf_op jit(solution)/shard_map/strip/all_to_all | solution.py:161
  20.1 5.2 %collective-permute-start = (bf16[8,144,128]{2,1,0:T(8,128)(2,1)S(1)}, bf16[8,144,128]{2,1,0:T(8,128)(2,1)S(1)}, u32[]{:S(2)}, u32[]{:S(2)}) collective-permute-start(bf16[8,144,128]{2,1,0:T(8,128)(2,1)S(1)} %all_to_all.25.g_ref.own_ref), channel_id=1, source_target_pairs={{0,4},{4,0},{1,5},{5,1},{2,6},{6,2},{3,7},{7,3},{8,12},{12,8},{9,1... | collective-permute-start | bytes 884744 | tf_op jit(solution)/shard_map/clips/ppermute | solution.py:163
  25.4 0.0 copy-done
  25.4 0.9 input_part.1
  26.3 0.2 collective-permute-done.pair_ref
  26.6 0.7 pad_maximum_fusion
  27.3 4.0 %all-to-all-start.1 = ((bf16[4,288,128]{2,1,0:T(8,128)(2,1)}), bf16[4,288,128]{2,1,0:T(8,128)(2,1)S(1)}, u32[]{:S(2)}, u32[]{:S(2)}) async-start(bf16[4,288,128]{2,1,0:T(8,128)(2,1)} %pad_maximum_fusion), calls=%async_computation.1 | async-start | bytes 589824 | tf_op jit(solution)/shard_map/filters/all_to_all | solution.py:181
  31.4 4.0 %collective-permute-start.1 = (bf16[2,8,2,8,128]{4,3,2,1,0:T(8,128)(2,1)S(1)}, bf16[2,8,2,8,128]{4,3,2,1,0:T(8,128)(2,1)S(1)}, u32[]{:S(2)}, u32[]{:S(2)}) collective-permute-start(bf16[2,8,2,8,128]{4,3,2,1,0:T(8,128)(2,1)S(1)} %fusion.4), channel_id=1, source_target_pairs={{64,0},{128,64},{192,128},{256,192},{320,256},{384,320},{448,384},... | collective-permute-start | bytes 196616 | tf_op jit(solution)/shard_map/edges/ppermute | solution.py:177
  35.4 0.1 pad_add_fusion.place_ref
  35.4 1.2 %collective-permute-done.1.edge_ref = bf16[2,8,2,8,128]{4,3,2,1,0:T(8,128)(2,1)S(1)} collective-permute-done((bf16[2,8,2,8,128]{4,3,2,1,0:T(8,128)(2,1)S(1)}, bf16[2,8,2,8,128]{4,3,2,1,0:T(8,128)(2,1)S(1)}, u32[]{:S(2)}, u32[]{:S(2)}) %collective-permute-start.1) | collective-permute-done | bytes 65568 | tf_op jit(solution)/shard_map/edges/ppermute | solution.py:177
  36.7 0.8 all-to-all-done.1.got_ref
  37.5 1.5 %weight_part.1 = (f32[8,64,128]{2,1,0:T(8,128)S(1)}, f32[64,128]{1,0:T(8,128)S(1)}) custom-call(s32[2]{0:T(128)S(1)} %pad_add_fusion.place_ref, bf16[8,144,128]{2,1,0:T(8,128)(2,1)S(1)} %all_to_all.25.g_ref.own_ref, bf16[8,144,128]{2,1,0:T(8,128)(2,1)S(1)} %collective-permute-done.pair_ref, bf16[2,8,2,8,128]{4,3,2,1,0:T(8,128)(2,1)S(1)} %collective-permute-done.1.edge_ref, ...), custom_call_target="tpu_custom_call" | custom-call | tf_op jit(solution)/shard_map/weight_part/pallas_call | solution.py:183
  39.0 19.9 %all_to_all.26 = f32[8,64,128]{2,1,0:T(8,128)S(1)} all-to-all(f32[8,64,128]{2,1,0:T(8,128)S(1)} %get-tuple-element.5), channel_id=1, replica_groups=mesh['z'=8,'y'=8,'core'=2,'x'=4] {'z'}, dimensions={0} | all-to-all | bytes 524288 | tf_op jit(solution)/shard_map/weight_sum/all_to_all | solution.py:195
  59.0 14.7 %all_to_all.27 = bf16[16,56,128]{2,1,0:T(8,128)(2,1)S(1)} all-to-all(bf16[16,56,128]{2,1,0:T(8,128)(2,1)S(1)} %broadcast_in_dim.26), channel_id=1, replica_groups={{0,16,32,48,128,144,160,176,256,272,288,304,384,400,416,432},{4,20,36,5..., dimensions={0} | all-to-all | bytes 458752 | tf_op jit(solution)/shard_map/gather_far/all_to_all | solution.py:199
  73.7 0.1 broadcast_in_dim.27
  73.8 13.3 %all_to_all.28 = bf16[4,16,56,128]{3,2,1,0:T(8,128)(2,1)S(1)} all-to-all(bf16[4,16,56,128]{3,2,1,0:T(8,128)(2,1)S(1)} %broadcast_in_dim.27), channel_id=1, replica_groups={{0,8,64,72},{148,140,84,76},{16,24,80,88},{164,156,100,92},{32,40,96,10..., dimensions={0} | all-to-all | bytes 1835008 | tf_op jit(solution)/shard_map/gather_near/all_to_all | solution.py:203
  87.1 0.2 copy.21
  87.4 4.2 %collective-permute-start.2 = (bf16[14,256,128]{2,1,0:T(8,128)(2,1)S(1)}, bf16[14,256,128]{2,1,0:T(8,128)(2,1)S(1)}, u32[]{:S(2)}, u32[]{:S(2)}) collective-permute-start(bf16[14,256,128]{2,1,0:T(8,128)(2,1)S(1)} %bitcast.38), channel_id=1, source_target_pairs={{0,4},{4,0},{1,5},{5,1},{2,6},{6,2},{3,7},{7,3},{8,12},{12,8},{9,1... | collective-permute-start | bytes 2752520 | tf_op jit(solution)/shard_map/swap/ppermute | solution.py:210
  91.7 0.1 concatenate.28
  91.8 0.1 select_reduce_fusion.1
  91.9 0.1 concatenate.27
  91.9 0.1 concatenate.29
  92.0 0.6 maximum_bitcast_fusion.1
  92.7 1.0 %collective-permute-done.2 = bf16[14,256,128]{2,1,0:T(8,128)(2,1)S(1)} collective-permute-done((bf16[14,256,128]{2,1,0:T(8,128)(2,1)S(1)}, bf16[14,256,128]{2,1,0:T(8,128)(2,1)S(1)}, u32[]{:S(2)}, u32[]{:S(2)}) %collective-permute-start.2) | collective-permute-done | bytes 917536 | tf_op jit(solution)/shard_map/swap/ppermute | solution.py:210
  93.7 0.1 broadcast_select_fusion
  94.2 0.0 copy-start.1
  94.2 1.2 %copy-done.1 = bf16[27,256,128]{2,1,0:T(8,128)(2,1)} copy-done((bf16[27,256,128]{2,1,0:T(8,128)(2,1)}, bf16[27,256,128]{2,1,0:T(8,128)(2,1)S(1)}, u32[]{:S(2)}) %copy-start.1) | copy-done | bytes 1769496
  (27 shorter events, 0.5 us)
Async XLA Ops:
  0.6 24.7 %copy-start = (bf16[3,3,3,256,128]{4,3,2,1,0:T(8,128)(2,1)S(1)}, bf16[3,3,3,256,128]{4,3,2,1,0:T(8,128)(2,1)}, u32[]{:S(2)}) copy-start(bf16[3,3,3,256,128]{4,3,2,1,0:T(8,128)(2,1)} %param.5) | copy-start | bytes 5308420
  20.1 6.4 %collective-permute-start = (bf16[8,144,128]{2,1,0:T(8,128)(2,1)S(1)}, bf16[8,144,128]{2,1,0:T(8,128)(2,1)S(1)}, u32[]{:S(2)}, u32[]{:S(2)}) collective-permute-start(bf16[8,144,128]{2,1,0:T(8,128)(2,1)S(1)} %all_to_all.25.g_ref.own_ref), channel_id=1, source_target_pairs={{0,4},{4,0},{1,5},{5,1},{2,6},{6,2},{3,7},{7,3},{8,12},{12,8},{9,1... | collective-permute-start | bytes 884744 | tf_op jit(solution)/shard_map/clips/ppermute | solution.py:163
  27.3 10.2 %all-to-all-start.1 = ((bf16[4,288,128]{2,1,0:T(8,128)(2,1)}), bf16[4,288,128]{2,1,0:T(8,128)(2,1)S(1)}, u32[]{:S(2)}, u32[]{:S(2)}) async-start(bf16[4,288,128]{2,1,0:T(8,128)(2,1)} %pad_maximum_fusion), calls=%async_computation.1 | async-start | bytes 589824 | tf_op jit(solution)/shard_map/filters/all_to_all | solution.py:181
  31.4 5.3 %collective-permute-start.1 = (bf16[2,8,2,8,128]{4,3,2,1,0:T(8,128)(2,1)S(1)}, bf16[2,8,2,8,128]{4,3,2,1,0:T(8,128)(2,1)S(1)}, u32[]{:S(2)}, u32[]{:S(2)}) collective-permute-start(bf16[2,8,2,8,128]{4,3,2,1,0:T(8,128)(2,1)S(1)} %fusion.4), channel_id=1, source_target_pairs={{64,0},{128,64},{192,128},{256,192},{320,256},{384,320},{448,384},... | collective-permute-start | bytes 196616 | tf_op jit(solution)/shard_map/edges/ppermute | solution.py:177
  87.4 6.3 %collective-permute-start.2 = (bf16[14,256,128]{2,1,0:T(8,128)(2,1)S(1)}, bf16[14,256,128]{2,1,0:T(8,128)(2,1)S(1)}, u32[]{:S(2)}, u32[]{:S(2)}) collective-permute-start(bf16[14,256,128]{2,1,0:T(8,128)(2,1)S(1)} %bitcast.38), channel_id=1, source_target_pairs={{0,4},{4,0},{1,5},{5,1},{2,6},{6,2},{3,7},{7,3},{8,12},{12,8},{9,1... | collective-permute-start | bytes 2752520 | tf_op jit(solution)/shard_map/swap/ppermute | solution.py:210
  94.2 1.2 %copy-start.1 = (bf16[27,256,128]{2,1,0:T(8,128)(2,1)}, bf16[27,256,128]{2,1,0:T(8,128)(2,1)S(1)}, u32[]{:S(2)}) copy-start(bf16[27,256,128]{2,1,0:T(8,128)(2,1)S(1)} %slice_dynamic-update-slice_fusion) | copy-start | bytes 5308420

commit v4 on v3

--- a/solution.py
+++ b/solution.py
@@ -89,7 +89,12 @@
         out_ref[i, EXT:, :] = (value - high.astype(jnp.float32)).astype(jnp.bfloat16)
 
 
-def weight_kernel(place_ref, own_ref, pair_ref, edge_ref, got_ref, out_ref, inner_ref, mid_ref):
+def split(prod):
+    half = NX * CJ
+    return prod[:half, CO:], prod[:half, :CO] + prod[half:, CO:], prod[half:, :CO]
+
+
+def weight_kernel(place_ref, own_ref, pair_ref, got_ref, out_ref, inner_ref, edge_ref, mid_ref):
     core, row = place_ref[0], place_ref[1]
     terms = got_ref[:, :TERMS, :].astype(jnp.float32)
     terms = terms[:, :EXT, :] + terms[:, EXT:, :]
@@ -99,27 +104,48 @@
         up = jnp.where(row - 1 == z, terms[:W], 0.0)
         out_ref[z, CHUNK:, :] = jnp.where(row + 1 == z, terms[EXT - W :], up)
 
-    x = got_ref[:, TERMS:, :].astype(jnp.float32).reshape(NX, NC, NY, CJ, F * H * W)
-    frames = []
+    x = got_ref[:, TERMS:, :].astype(jnp.float32)
+    cell = lax.broadcasted_iota(jnp.int32, x.shape, 2) % (H * W)
+    down = jnp.where(cell < W, 0.0, pltpu.roll(x, W, 2))
+    up = jnp.where(cell >= (H - 1) * W, 0.0, pltpu.roll(x, F * H * W - W, 2))
+    side = jnp.where(core == 0, down, up)
+    shape = (NX, NC, NY, CJ, F * H * W)
+    stack = []
+    for value in (x.reshape(shape), side.reshape(shape)):
+        for f in range(F):
+            cut = slice(f * H * W, (f + 1) * H * W)
+            cols = [
+                value[:, clip, y, :, cut].reshape(NX * CJ, H * W)
+                for clip in range(NC)
+                for y in range(NY)
+            ]
+            stack.append(jnp.concatenate(cols, axis=1))
+    xs = jnp.concatenate(stack, axis=0).astype(jnp.bfloat16)
+    outer = x.reshape(shape)
     for f in range(F):
-        cut = slice(f * H * W, (f + 1) * H * W)
+        first, last = f * H * W, (f + 1) * H * W - W
         cols = [
-            x[:, clip, y, :, cut].reshape(NX * CJ, H * W) for clip in range(NC) for y in range(NY)
+            jnp.where(
+                core == 0,
+                outer[:, clip, y, :, last : last + W],
+                outer[:, clip, y, :, first : first + W],
+            ).reshape(NX * CJ, W)
+            for clip in range(NC)
+            for y in range(NY)
         ]
-        frames.append(jnp.concatenate(cols, axis=1))
-    xs = jnp.concatenate(frames, axis=0).astype(jnp.bfloat16)
+        edge_ref[f * NX * CJ : (f + 1) * NX * CJ, :] = jnp.concatenate(cols, axis=1).astype(jnp.bfloat16)
     half = NX * CJ
-    mids, sides = [], []
-    for clip, ref in enumerate((own_ref, pair_ref)):
-        rows = ref[:, :GROWS, :].astype(jnp.float32).reshape(NY, F, H, W, CO)
-        edge = edge_ref[clip].astype(jnp.float32).reshape(NY, F, 1, W, CO)
-        below = jnp.concatenate([rows[:, :, 1:], edge], axis=2)
-        above = jnp.concatenate([edge, rows[:, :, :-1]], axis=2)
-        mids.append(rows.reshape(NY, F * H, W, CO))
-        sides.append(jnp.where(core == 0, below, above).reshape(NY, F * H, W, CO))
+    clips = [
+        ref[:, :GROWS, :].astype(jnp.float32).reshape(NY, F * H, W, CO) for ref in (own_ref, pair_ref)
+    ]
     border = jnp.zeros((1, F * H, W, CO), jnp.float32)
 
-    def product(clips, te):
+    def put(slot, value):
+        group, t = divmod(slot, 7)
+        for q in range(NX):
+            out_ref[group * NX + q, t * CJ : (t + 1) * CJ, :] = value[q * CJ : (q + 1) * CJ]
+
+    for te in range(3):
         cols = [[], []]
         for rows in clips:
             left = jnp.concatenate([border, rows[:-1]], axis=0)
@@ -129,21 +155,33 @@
                 cols[f].append(moved[:, f].reshape(NY * H * W, CO))
         both = [jnp.concatenate(c, axis=0).astype(jnp.bfloat16) for c in cols]
         prod = jnp.dot(xs, jnp.concatenate(both, axis=1), preferred_element_type=jnp.float32)
-        return prod[:half, CO:], prod[:half, :CO] + prod[half:, CO:], prod[half:, :CO]
-
-    def put(slot, value):
-        group, t = divmod(slot, 7)
-        for q in range(NX):
-            out_ref[group * NX + q, t * CJ : (t + 1) * CJ, :] = value[q * CJ : (q + 1) * CJ]
-
-    for te in range(3):
-        for ta, value in enumerate(product(sides, te)):
+        for ta, value in enumerate(split(prod[: 2 * half])):
+            mid_ref[ta * 3 + te] = value
+        for ta, value in enumerate(split(prod[2 * half :])):
             put(ta * 3 + te, value)
-        for ta, value in enumerate(product(mids, te)):
-            mid_ref[ta * 3 + te] = value
     mid_ref[9] = jnp.zeros((half, CO), jnp.float32)
     for i in range(5):
         put(9 + i, mid_ref[i + 5 * core])
+
+
+def edge_kernel(x_ref, g_ref, acc_ref, out_ref):
+    out_ref[...] = acc_ref[...]
+    border = jnp.zeros((1, F, W, CO), jnp.float32)
+    for te in range(3):
+        cols = [[], []]
+        for clip in range(NC):
+            rows = g_ref[clip].astype(jnp.float32)
+            left = jnp.concatenate([border, rows[:-1]], axis=0)
+            right = jnp.concatenate([rows[1:], border], axis=0)
+            moved = shifted(rows, left, right, te)
+            for f in range(F):
+                cols[f].append(moved[:, f].reshape(NY * W, CO))
+        both = [jnp.concatenate(c, axis=0).astype(jnp.bfloat16) for c in cols]
+        prod = jnp.dot(x_ref[...], jnp.concatenate(both, axis=1), preferred_element_type=jnp.float32)
+        for ta, value in enumerate(split(prod)):
+            group, t = divmod(ta * 3 + te, 7)
+            for q in range(NX):
+                out_ref[group * NX + q, t * CJ : (t + 1) * CJ, :] += value[q * CJ : (q + 1) * CJ]
 
 
 def shards(activations, out_grad, kernel):
@@ -180,17 +218,27 @@
         xmine = jnp.broadcast_to(jnp.concatenate(xmine, axis=0), (NX, NC * NY * CJ, F * H * W))
         got = lax.all_to_all(jnp.concatenate([terms, xmine], axis=1), "x", 0, 0, tiled=True)
     with jax.named_scope("weight_part"):
-        local, inner = pl.pallas_call(
+        local, inner, outer = pl.pallas_call(
             weight_kernel,
             out_shape=[
                 jax.ShapeDtypeStruct((NZ, CHUNK + W, CO), jnp.float32),
                 jax.ShapeDtypeStruct((H * W, F * CI), jnp.float32),
+                jax.ShapeDtypeStruct((F * NX * CJ, NC * NY * W), jnp.bfloat16),
             ],
-            in_specs=[smem] + [vmem] * 4,
-            out_specs=[vmem] * 2,
+            in_specs=[smem] + [vmem] * 3,
+            out_specs=[vmem] * 3,
             scratch_shapes=[pltpu.VMEM((10, NX * CJ, CO), jnp.float32)],
             compiler_params=params,
-        )(jnp.stack([core, row]), strip, pair, edge, got)
+        )(jnp.stack([core, row]), strip, pair, got)
+    with jax.named_scope("weight_edge"):
+        local = pl.pallas_call(
+            edge_kernel,
+            out_shape=jax.ShapeDtypeStruct(local.shape, jnp.float32),
+            in_specs=[vmem] * 3,
+            out_specs=vmem,
+            input_output_aliases={2: 0},
+            compiler_params=params,
+        )(outer, edge, local)
     with jax.named_scope("weight_sum"):
         shares = lax.all_to_all(local, "z", 0, 0, tiled=True)
         scale = 1.0 / math.sqrt(NZ * NY * NC * F * H * W)

time: 95.8 us -> 95.1 us (level)
  blocking collectives: 65.6 us -> 64.5 us
    all_to_all x1, waiting for transfers between devices: 0.78 us -> 2.02 us  [shards(): lax.all_to_all(jnp.concatenate([terms, xmine], axis=1), 'x', 0, 0, tiled=...]
    ppermute x1, waiting for transfers between devices: 1.23 us -> 0.01 us  [shards(): edge = lax.ppermute(edge, ('z', 'core'), route)]
  transfers between devices with their start and end apart: 4 -> 4, of which waited for: 4 -> 3; matrix products, arithmetic and copies ran while one was open for 1% -> 1% of each run, Pallas kernels for 1% -> 2%
where the time goes in v4:
time: 95.1 us; the launch traced here: 94.7 us
  blocking collectives  64.5 us (68%)
  starting transfers between devices  18 us (19%)
  local copies, waits for them, and re-layouts  3.94 us (4%)
  waiting for transfers between devices  3.27 us (3%)
  Pallas kernels  2.34 us (2%)
  other arithmetic  1.74 us (2%)
    all_to_all x1, blocking collectives, shards(): shares = lax.all_to_all(local, 'z', 0, 0, tiled=True)  19.1 us
    all_to_all x1, blocking collectives, shards(): lax.all_to_all(jnp.concatenate([rows, xt], axis=1), 'y', 0, 0, tiled=True)  17.6 us
    all_to_all x1, blocking collectives, shards(): lax.all_to_all(jnp.broadcast_to(mine, (16, CHUNK, CO)), TILE, 0, 0, axis_...  14.5 us
    all_to_all x1, blocking collectives, shards(): lax.all_to_all(jnp.broadcast_to(far, (4, 16, CHUNK, CO)), TILE, 0, 0, axi...  13.4 us
    ppermute x1, starting transfers between devices, shards(): pair = lax.ppermute(strip, 'core', swap)  5.25 us
    ppermute x1, starting transfers between devices, shards(): other = lax.ppermute(half, 'core', swap)  4.72 us
    all_to_all x1, starting transfers between devices, shards(): lax.all_to_all(jnp.concatenate([terms, xmine], axis=1), 'x', 0, 0, tiled=...  4.01 us
    ppermute x1, starting transfers between devices, shards(): edge = lax.ppermute(edge, ('z', 'core'), route)  4 us
  transfers between devices with their start and end apart: 4, of which 3 were waited for; matrix products, arithmetic and copies ran while one was open for 1% of the time, Pallas kernels for 2%

profile of v4, /device:TPU:1, one launch (start us, length us, event | category | flops | bytes accessed | tf_op | source)
XLA Modules:
  0.0 94.7 jit_solution(5851946989892744570)
XLA Ops:
  0.6 0.0 copy-start
  0.6 1.0 %copy.16 = bf16[128,64]{0,1:T(8,128)(2,1)S(1)} copy(bf16[128,64]{1,0:T(8,128)(2,1)} %bitcast.44) | data formatting | bytes 32768 | tf_op jit(solution)/shard_map/strip/reshape;strip/squeeze | solution.py:196
  1.6 0.8 broadcast_in_dim.22
  2.4 17.6 %all_to_all.25.g_ref.own_ref = bf16[8,144,128]{2,1,0:T(8,128)(2,1)S(1)} all-to-all(bf16[8,144,128]{2,1,0:T(8,128)(2,1)S(1)} %fusion.1), channel_id=1, replica_groups=mesh['z'=8,'y'=8,'core'=2,'x'=4] {'y'}, dimensions={0} | all-to-all | bytes 589824 | tf_op jit(solution)/shard_map/strip/all_to_all | solution.py:199
  20.1 5.2 %collective-permute-start = (bf16[8,144,128]{2,1,0:T(8,128)(2,1)S(1)}, bf16[8,144,128]{2,1,0:T(8,128)(2,1)S(1)}, u32[]{:S(2)}, u32[]{:S(2)}) collective-permute-start(bf16[8,144,128]{2,1,0:T(8,128)(2,1)S(1)} %all_to_all.25.g_ref.own_ref), channel_id=1, source_target_pairs={{0,4},{4,0},{1,5},{5,1},{2,6},{6,2},{3,7},{7,3},{8,12},{12,8},{9,1... | collective-permute-start | bytes 884744 | tf_op jit(solution)/shard_map/clips/ppermute | solution.py:201
  25.4 0.0 copy-done
  25.4 0.9 input_part.1
  26.3 0.2 collective-permute-done.pair_ref
  26.6 0.7 pad_maximum_fusion
  27.3 4.0 %all-to-all-start.1 = ((bf16[4,288,128]{2,1,0:T(8,128)(2,1)}), bf16[4,288,128]{2,1,0:T(8,128)(2,1)S(1)}, u32[]{:S(2)}, u32[]{:S(2)}) async-start(bf16[4,288,128]{2,1,0:T(8,128)(2,1)} %pad_maximum_fusion), calls=%async_computation.1 | async-start | bytes 589824 | tf_op jit(solution)/shard_map/filters/all_to_all | solution.py:219
  31.4 4.0 %collective-permute-start.1 = (bf16[2,8,2,8,128]{4,3,2,1,0:T(8,128)(2,1)S(1)}, bf16[2,8,2,8,128]{4,3,2,1,0:T(8,128)(2,1)S(1)}, u32[]{:S(2)}, u32[]{:S(2)}) collective-permute-start(bf16[2,8,2,8,128]{4,3,2,1,0:T(8,128)(2,1)S(1)} %fusion.4), channel_id=1, source_target_pairs={{64,0},{128,64},{192,128},{256,192},{320,256},{384,320},{448,384},... | collective-permute-start | bytes 196616 | tf_op jit(solution)/shard_map/edges/ppermute | solution.py:215
  35.4 0.1 pad_add_fusion.place_ref
  35.4 2.0 %all-to-all-done.1.got_ref = bf16[4,288,128]{2,1,0:T(8,128)(2,1)S(1)} async-done(((bf16[4,288,128]{2,1,0:T(8,128)(2,1)}), bf16[4,288,128]{2,1,0:T(8,128)(2,1)S(1)}, u32[]{:S(2)}, u32[]{:S(2)}) %all-to-all-start.1) | async-done | bytes 294944 | tf_op jit(solution)/shard_map/filters/all_to_all | solution.py:219
  37.5 1.2 %weight_part.1 = (f32[8,64,128]{2,1,0:T(8,128)S(1)}, f32[64,128]{1,0:T(8,128)S(1)}, bf16[64,128]{1,0:T(8,128)(2,1)S(1)}) custom-call(s32[2]{0:T(128)S(1)} %pad_add_fusion.place_ref, bf16[8,144,128]{2,1,0:T(8,128)(2,1)S(1)} %all_to_all.25.g_ref.own_ref, bf16[8,144,128]{2,1,0:T(8,128)(2,1)S(1)} %collective-permute-done.pair_ref, ...), custom_call_target="tpu_custom_call" | custom-call | tf_op jit(solution)/shard_map/weight_part/pallas_call | solution.py:221
  38.7 0.0 collective-permute-done.1.g_ref
  38.7 0.2 weight_edge.1
  38.9 19.1 %all_to_all.26 = f32[8,64,128]{2,1,0:T(8,128)S(1)} all-to-all(f32[8,64,128]{2,1,0:T(8,128)S(1)} %weight_edge.1), channel_id=1, replica_groups=mesh['z'=8,'y'=8,'core'=2,'x'=4] {'z'}, dimensions={0} | all-to-all | bytes 524288 | tf_op jit(solution)/shard_map/weight_sum/all_to_all | solution.py:243
  58.0 14.5 %all_to_all.27 = bf16[16,56,128]{2,1,0:T(8,128)(2,1)S(1)} all-to-all(bf16[16,56,128]{2,1,0:T(8,128)(2,1)S(1)} %broadcast_in_dim.26), channel_id=1, replica_groups={{0,16,32,48,128,144,160,176,256,272,288,304,384,400,416,432},{4,20,36,5..., dimensions={0} | all-to-all | bytes 458752 | tf_op jit(solution)/shard_map/gather_far/all_to_all | solution.py:247
  72.5 0.1 broadcast_in_dim.27
  72.6 13.4 %all_to_all.28 = bf16[4,16,56,128]{3,2,1,0:T(8,128)(2,1)S(1)} all-to-all(bf16[4,16,56,128]{3,2,1,0:T(8,128)(2,1)S(1)} %broadcast_in_dim.27), channel_id=1, replica_groups={{0,8,64,72},{148,140,84,76},{16,24,80,88},{164,156,100,92},{32,40,96,10..., dimensions={0} | all-to-all | bytes 1835008 | tf_op jit(solution)/shard_map/gather_near/all_to_all | solution.py:251
  86.0 0.2 copy.22
  86.2 4.7 %collective-permute-start.2 = (bf16[14,256,128]{2,1,0:T(8,128)(2,1)S(1)}, bf16[14,256,128]{2,1,0:T(8,128)(2,1)S(1)}, u32[]{:S(2)}, u32[]{:S(2)}) collective-permute-start(bf16[14,256,128]{2,1,0:T(8,128)(2,1)S(1)} %bitcast.38), channel_id=1, source_target_pairs={{0,4},{4,0},{1,5},{5,1},{2,6},{6,2},{3,7},{7,3},{8,12},{12,8},{9,1... | collective-permute-start | bytes 2752520 | tf_op jit(solution)/shard_map/swap/ppermute | solution.py:258
  91.0 0.1 concatenate.28
  91.1 0.1 select_reduce_fusion.1
  91.2 0.1 concatenate.27
  91.3 0.1 concatenate.29
  91.4 0.6 maximum_bitcast_fusion.1
  92.0 1.0 %collective-permute-done.2 = bf16[14,256,128]{2,1,0:T(8,128)(2,1)S(1)} collective-permute-done((bf16[14,256,128]{2,1,0:T(8,128)(2,1)S(1)}, bf16[14,256,128]{2,1,0:T(8,128)(2,1)S(1)}, u32[]{:S(2)}, u32[]{:S(2)}) %collective-permute-start.2) | collective-permute-done | bytes 917536 | tf_op jit(solution)/shard_map/swap/ppermute | solution.py:258
  93.0 0.1 broadcast_select_fusion
  93.5 0.0 copy-start.1
  93.5 1.2 %copy-done.1 = bf16[27,256,128]{2,1,0:T(8,128)(2,1)} copy-done((bf16[27,256,128]{2,1,0:T(8,128)(2,1)}, bf16[27,256,128]{2,1,0:T(8,128)(2,1)S(1)}, u32[]{:S(2)}) %copy-start.1) | copy-done | bytes 1769496
  (27 shorter events, 0.5 us)
Async XLA Ops:
  0.6 24.7 %copy-start = (bf16[3,3,3,256,128]{4,3,2,1,0:T(8,128)(2,1)S(1)}, bf16[3,3,3,256,128]{4,3,2,1,0:T(8,128)(2,1)}, u32[]{:S(2)}) copy-start(bf16[3,3,3,256,128]{4,3,2,1,0:T(8,128)(2,1)} %param.5) | copy-start | bytes 5308420
  20.1 6.4 %collective-permute-start = (bf16[8,144,128]{2,1,0:T(8,128)(2,1)S(1)}, bf16[8,144,128]{2,1,0:T(8,128)(2,1)S(1)}, u32[]{:S(2)}, u32[]{:S(2)}) collective-permute-start(bf16[8,144,128]{2,1,0:T(8,128)(2,1)S(1)} %all_to_all.25.g_ref.own_ref), channel_id=1, source_target_pairs={{0,4},{4,0},{1,5},{5,1},{2,6},{6,2},{3,7},{7,3},{8,12},{12,8},{9,1... | collective-permute-start | bytes 884744 | tf_op jit(solution)/shard_map/clips/ppermute | solution.py:201
  27.3 10.2 %all-to-all-start.1 = ((bf16[4,288,128]{2,1,0:T(8,128)(2,1)}), bf16[4,288,128]{2,1,0:T(8,128)(2,1)S(1)}, u32[]{:S(2)}, u32[]{:S(2)}) async-start(bf16[4,288,128]{2,1,0:T(8,128)(2,1)} %pad_maximum_fusion), calls=%async_computation.1 | async-start | bytes 589824 | tf_op jit(solution)/shard_map/filters/all_to_all | solution.py:219
  31.4 7.3 %collective-permute-start.1 = (bf16[2,8,2,8,128]{4,3,2,1,0:T(8,128)(2,1)S(1)}, bf16[2,8,2,8,128]{4,3,2,1,0:T(8,128)(2,1)S(1)}, u32[]{:S(2)}, u32[]{:S(2)}) collective-permute-start(bf16[2,8,2,8,128]{4,3,2,1,0:T(8,128)(2,1)S(1)} %fusion.4), channel_id=1, source_target_pairs={{64,0},{128,64},{192,128},{256,192},{320,256},{384,320},{448,384},... | collective-permute-start | bytes 196616 | tf_op jit(solution)/shard_map/edges/ppermute | solution.py:215
  86.2 6.8 %collective-permute-start.2 = (bf16[14,256,128]{2,1,0:T(8,128)(2,1)S(1)}, bf16[14,256,128]{2,1,0:T(8,128)(2,1)S(1)}, u32[]{:S(2)}, u32[]{:S(2)}) collective-permute-start(bf16[14,256,128]{2,1,0:T(8,128)(2,1)S(1)} %bitcast.38), channel_id=1, source_target_pairs={{0,4},{4,0},{1,5},{5,1},{2,6},{6,2},{3,7},{7,3},{8,12},{12,8},{9,1... | collective-permute-start | bytes 2752520 | tf_op jit(solution)/shard_map/swap/ppermute | solution.py:258
  93.5 1.2 %copy-start.1 = (bf16[27,256,128]{2,1,0:T(8,128)(2,1)}, bf16[27,256,128]{2,1,0:T(8,128)(2,1)S(1)}, u32[]{:S(2)}) copy-start(bf16[27,256,128]{2,1,0:T(8,128)(2,1)S(1)} %slice_dynamic-update-slice_fusion) | copy-start | bytes 5308420

commit v5 on v4

--- a/solution.py
+++ b/solution.py
@@ -17,7 +17,7 @@
 GROWS = F * H * W
 EXT = (H + 2) * W
 CJ = CI // NY
-XROWS = 16
+XROWS = CJ
 TERMS = 2 * EXT
 CHUNK = 7 * CJ
 

time: 95.1 us -> 94.8 us (level)
  no operation moved by 1% of the time
where the time goes in v5:
time: 94.8 us; the launch traced here: 94.3 us
  blocking collectives  64 us (68%)
  starting transfers between devices  18.2 us (19%)
  local copies, waits for them, and re-layouts  3.94 us (4%)
  waiting for transfers between devices  3.24 us (3%)
  Pallas kernels  2.34 us (2%)
  other arithmetic  1.74 us (2%)
    all_to_all x1, blocking collectives, shards(): shares = lax.all_to_all(local, 'z', 0, 0, tiled=True)  19.1 us
    all_to_all x1, blocking collectives, shards(): lax.all_to_all(jnp.concatenate([rows, xt], axis=1), 'y', 0, 0, tiled=True)  17.2 us
    all_to_all x1, blocking collectives, shards(): lax.all_to_all(jnp.broadcast_to(mine, (16, CHUNK, CO)), TILE, 0, 0, axis_...  14.5 us
    all_to_all x1, blocking collectives, shards(): lax.all_to_all(jnp.broadcast_to(far, (4, 16, CHUNK, CO)), TILE, 0, 0, axi...  13.3 us
    ppermute x1, starting transfers between devices, shards(): pair = lax.ppermute(strip, 'core', swap)  5.38 us
    ppermute x1, starting transfers between devices, shards(): other = lax.ppermute(half, 'core', swap)  4.81 us
    all_to_all x1, starting transfers between devices, shards(): lax.all_to_all(jnp.concatenate([terms, xmine], axis=1), 'x', 0, 0, tiled=...  4.01 us
    ppermute x1, starting transfers between devices, shards(): edge = lax.ppermute(edge, ('z', 'core'), route)  4 us
  transfers between devices with their start and end apart: 4, of which 3 were waited for; matrix products, arithmetic and copies ran while one was open for 1% of the time, Pallas kernels for 2%

profile of v5, /device:TPU:1, one launch (start us, length us, event | category | flops | bytes accessed | tf_op | source)
XLA Modules:
  0.0 94.3 jit_solution(1792604671590521093)
XLA Ops:
  0.6 0.0 copy-start
  0.6 1.0 %copy.16 = bf16[128,64]{0,1:T(8,128)(2,1)S(1)} copy(bf16[128,64]{1,0:T(8,128)(2,1)} %bitcast.44) | data formatting | bytes 32768 | tf_op jit(solution)/shard_map/strip/reshape;strip/squeeze | solution.py:196
  1.6 0.8 broadcast_in_dim.22
  2.4 17.2 %all_to_all.25.g_ref.own_ref = bf16[8,136,128]{2,1,0:T(8,128)(2,1)S(1)} all-to-all(bf16[8,136,128]{2,1,0:T(8,128)(2,1)S(1)} %pad_maximum_fusion.1), channel_id=1, replica_groups=mesh['z'=8,'y'=8,'core'=2,'x'=4] {'y'}, dimensions={0} | all-to-all | bytes 557056 | tf_op jit(solution)/shard_map/strip/all_to_all | solution.py:199
  19.6 5.4 %collective-permute-start = (bf16[8,136,128]{2,1,0:T(8,128)(2,1)S(1)}, bf16[8,136,128]{2,1,0:T(8,128)(2,1)S(1)}, u32[]{:S(2)}, u32[]{:S(2)}) collective-permute-start(bf16[8,136,128]{2,1,0:T(8,128)(2,1)S(1)} %all_to_all.25.g_ref.own_ref), channel_id=1, source_target_pairs={{0,4},{4,0},{1,5},{5,1},{2,6},{6,2},{3,7},{7,3},{8,12},{12,8},{9,1... | collective-permute-start | bytes 835592 | tf_op jit(solution)/shard_map/clips/ppermute | solution.py:201
  25.0 0.0 copy-done
  25.0 0.9 input_part.1
  26.0 0.2 collective-permute-done.pair_ref
  26.2 0.7 pad_maximum_fusion
  26.9 4.0 %all-to-all-start.1 = ((bf16[4,288,128]{2,1,0:T(8,128)(2,1)}), bf16[4,288,128]{2,1,0:T(8,128)(2,1)S(1)}, u32[]{:S(2)}, u32[]{:S(2)}) async-start(bf16[4,288,128]{2,1,0:T(8,128)(2,1)} %pad_maximum_fusion), calls=%async_computation.1 | async-start | bytes 589824 | tf_op jit(solution)/shard_map/filters/all_to_all | solution.py:219
  31.0 4.0 %collective-permute-start.1 = (bf16[2,8,2,8,128]{4,3,2,1,0:T(8,128)(2,1)S(1)}, bf16[2,8,2,8,128]{4,3,2,1,0:T(8,128)(2,1)S(1)}, u32[]{:S(2)}, u32[]{:S(2)}) collective-permute-start(bf16[2,8,2,8,128]{4,3,2,1,0:T(8,128)(2,1)S(1)} %fusion.2), channel_id=1, source_target_pairs={{64,0},{128,64},{192,128},{256,192},{320,256},{384,320},{448,384},... | collective-permute-start | bytes 196616 | tf_op jit(solution)/shard_map/edges/ppermute | solution.py:215
  35.0 0.1 pad_add_fusion.place_ref
  35.1 2.0 %all-to-all-done.1.got_ref = bf16[4,288,128]{2,1,0:T(8,128)(2,1)S(1)} async-done(((bf16[4,288,128]{2,1,0:T(8,128)(2,1)}), bf16[4,288,128]{2,1,0:T(8,128)(2,1)S(1)}, u32[]{:S(2)}, u32[]{:S(2)}) %all-to-all-start.1) | async-done | bytes 294944 | tf_op jit(solution)/shard_map/filters/all_to_all | solution.py:219
  37.1 1.2 %weight_part.1 = (f32[8,64,128]{2,1,0:T(8,128)S(1)}, f32[64,128]{1,0:T(8,128)S(1)}, bf16[64,128]{1,0:T(8,128)(2,1)S(1)}) custom-call(s32[2]{0:T(128)S(1)} %pad_add_fusion.place_ref, bf16[8,136,128]{2,1,0:T(8,128)(2,1)S(1)} %all_to_all.25.g_ref.own_ref, bf16[8,136,128]{2,1,0:T(8,128)(2,1)S(1)} %collective-permute-done.pair_ref, ...), custom_call_target="tpu_custom_call" | custom-call | tf_op jit(solution)/shard_map/weight_part/pallas_call | solution.py:221
  38.3 0.0 collective-permute-done.1.g_ref
  38.3 0.2 weight_edge.1
  38.5 19.1 %all_to_all.26 = f32[8,64,128]{2,1,0:T(8,128)S(1)} all-to-all(f32[8,64,128]{2,1,0:T(8,128)S(1)} %weight_edge.1), channel_id=1, replica_groups=mesh['z'=8,'y'=8,'core'=2,'x'=4] {'z'}, dimensions={0} | all-to-all | bytes 524288 | tf_op jit(solution)/shard_map/weight_sum/all_to_all | solution.py:243
  57.7 14.5 %all_to_all.27 = bf16[16,56,128]{2,1,0:T(8,128)(2,1)S(1)} all-to-all(bf16[16,56,128]{2,1,0:T(8,128)(2,1)S(1)} %broadcast_in_dim.26), channel_id=1, replica_groups={{0,16,32,48,128,144,160,176,256,272,288,304,384,400,416,432},{4,20,36,5..., dimensions={0} | all-to-all | bytes 458752 | tf_op jit(solution)/shard_map/gather_far/all_to_all | solution.py:247
  72.2 0.1 broadcast_in_dim.27
  72.3 13.3 %all_to_all.28 = bf16[4,16,56,128]{3,2,1,0:T(8,128)(2,1)S(1)} all-to-all(bf16[4,16,56,128]{3,2,1,0:T(8,128)(2,1)S(1)} %broadcast_in_dim.27), channel_id=1, replica_groups={{0,8,64,72},{148,140,84,76},{16,24,80,88},{164,156,100,92},{32,40,96,10..., dimensions={0} | all-to-all | bytes 1835008 | tf_op jit(solution)/shard_map/gather_near/all_to_all | solution.py:251
  85.5 0.2 copy.22
  85.8 4.8 %collective-permute-start.2 = (bf16[14,256,128]{2,1,0:T(8,128)(2,1)S(1)}, bf16[14,256,128]{2,1,0:T(8,128)(2,1)S(1)}, u32[]{:S(2)}, u32[]{:S(2)}) collective-permute-start(bf16[14,256,128]{2,1,0:T(8,128)(2,1)S(1)} %bitcast.38), channel_id=1, source_target_pairs={{0,4},{4,0},{1,5},{5,1},{2,6},{6,2},{3,7},{7,3},{8,12},{12,8},{9,1... | collective-permute-start | bytes 2752520 | tf_op jit(solution)/shard_map/swap/ppermute | solution.py:258
  90.6 0.1 concatenate.28
  90.7 0.1 select_reduce_fusion.1
  90.8 0.1 concatenate.27
  90.9 0.1 concatenate.29
  91.0 0.6 maximum_bitcast_fusion.1
  91.6 1.0 %collective-permute-done.2 = bf16[14,256,128]{2,1,0:T(8,128)(2,1)S(1)} collective-permute-done((bf16[14,256,128]{2,1,0:T(8,128)(2,1)S(1)}, bf16[14,256,128]{2,1,0:T(8,128)(2,1)S(1)}, u32[]{:S(2)}, u32[]{:S(2)}) %collective-permute-start.2) | collective-permute-done | bytes 917536 | tf_op jit(solution)/shard_map/swap/ppermute | solution.py:258
  92.7 0.1 broadcast_select_fusion
  93.1 0.0 copy-start.1
  93.1 1.2 %copy-done.1 = bf16[27,256,128]{2,1,0:T(8,128)(2,1)} copy-done((bf16[27,256,128]{2,1,0:T(8,128)(2,1)}, bf16[27,256,128]{2,1,0:T(8,128)(2,1)S(1)}, u32[]{:S(2)}) %copy-start.1) | copy-done | bytes 1769496
  (27 shorter events, 0.5 us)
Async XLA Ops:
  0.6 24.4 %copy-start = (bf16[3,3,3,256,128]{4,3,2,1,0:T(8,128)(2,1)S(1)}, bf16[3,3,3,256,128]{4,3,2,1,0:T(8,128)(2,1)}, u32[]{:S(2)}) copy-start(bf16[3,3,3,256,128]{4,3,2,1,0:T(8,128)(2,1)} %param.5) | copy-start | bytes 5308420
  19.6 6.5 %collective-permute-start = (bf16[8,136,128]{2,1,0:T(8,128)(2,1)S(1)}, bf16[8,136,128]{2,1,0:T(8,128)(2,1)S(1)}, u32[]{:S(2)}, u32[]{:S(2)}) collective-permute-start(bf16[8,136,128]{2,1,0:T(8,128)(2,1)S(1)} %all_to_all.25.g_ref.own_ref), channel_id=1, source_target_pairs={{0,4},{4,0},{1,5},{5,1},{2,6},{6,2},{3,7},{7,3},{8,12},{12,8},{9,1... | collective-permute-start | bytes 835592 | tf_op jit(solution)/shard_map/clips/ppermute | solution.py:201
  26.9 10.2 %all-to-all-start.1 = ((bf16[4,288,128]{2,1,0:T(8,128)(2,1)}), bf16[4,288,128]{2,1,0:T(8,128)(2,1)S(1)}, u32[]{:S(2)}, u32[]{:S(2)}) async-start(bf16[4,288,128]{2,1,0:T(8,128)(2,1)} %pad_maximum_fusion), calls=%async_computation.1 | async-start | bytes 589824 | tf_op jit(solution)/shard_map/filters/all_to_all | solution.py:219
  31.0 7.3 %collective-permute-start.1 = (bf16[2,8,2,8,128]{4,3,2,1,0:T(8,128)(2,1)S(1)}, bf16[2,8,2,8,128]{4,3,2,1,0:T(8,128)(2,1)S(1)}, u32[]{:S(2)}, u32[]{:S(2)}) collective-permute-start(bf16[2,8,2,8,128]{4,3,2,1,0:T(8,128)(2,1)S(1)} %fusion.2), channel_id=1, source_target_pairs={{64,0},{128,64},{192,128},{256,192},{320,256},{384,320},{448,384},... | collective-permute-start | bytes 196616 | tf_op jit(solution)/shard_map/edges/ppermute | solution.py:215
  85.8 6.9 %collective-permute-start.2 = (bf16[14,256,128]{2,1,0:T(8,128)(2,1)S(1)}, bf16[14,256,128]{2,1,0:T(8,128)(2,1)S(1)}, u32[]{:S(2)}, u32[]{:S(2)}) collective-permute-start(bf16[14,256,128]{2,1,0:T(8,128)(2,1)S(1)} %bitcast.38), channel_id=1, source_target_pairs={{0,4},{4,0},{1,5},{5,1},{2,6},{6,2},{3,7},{7,3},{8,12},{12,8},{9,1... | collective-permute-start | bytes 2752520 | tf_op jit(solution)/shard_map/swap/ppermute | solution.py:258
  93.1 1.2 %copy-start.1 = (bf16[27,256,128]{2,1,0:T(8,128)(2,1)}, bf16[27,256,128]{2,1,0:T(8,128)(2,1)S(1)}, u32[]{:S(2)}) copy-start(bf16[27,256,128]{2,1,0:T(8,128)(2,1)S(1)} %slice_dynamic-update-slice_fusion) | copy-start | bytes 5308420

commit v6 on v5

--- a/solution.py
+++ b/solution.py
@@ -50,8 +50,14 @@
     return jnp.where(row == 0, pltpu.roll(left, 1, axis), pltpu.roll(own, 1, axis))
 
 
-def input_kernel(col_ref, g_ref, k_ref, out_ref):
+def input_kernel(col_ref, g_ref, k_hbm, out_ref, k_ref, sems):
     col = col_ref[0]
+    copies = [
+        pltpu.make_async_copy(k_hbm.at[pl.ds(9 * ta, 9)], k_ref.at[pl.ds(9 * ta, 9)], sems.at[ta])
+        for ta in range(3)
+    ]
+    for copy in copies:
+        copy.start()
 
     def tile(i):
         return g_ref[i, :GROWS, :].astype(jnp.float32).reshape(F * H, W, CO)
@@ -61,6 +67,8 @@
     right = jnp.where(col < NY - 1, tile(jnp.minimum(col + 1, NY - 1)), 0.0)
     dims = (((1,), (1,)), ((), ()))
     sums = [[jnp.zeros((H * W, CIN), jnp.float32) for _ in range(3)] for _ in range(F)]
+    for copy in copies:
+        copy.wait()
     for te in range(3):
         rows = shifted(own, left, right, te).reshape(F, H * W, CO).astype(jnp.bfloat16)
         both = jnp.concatenate([rows[0], rows[1]], axis=1)
@@ -203,8 +211,9 @@
         terms = pl.pallas_call(
             input_kernel,
             out_shape=jax.ShapeDtypeStruct((NX, TERMS, F * CI), jnp.bfloat16),
-            in_specs=[smem, vmem, vmem],
+            in_specs=[smem, vmem, pl.BlockSpec(memory_space=pltpu.HBM)],
             out_specs=vmem,
+            scratch_shapes=[pltpu.VMEM((27, CIN, CO), jnp.bfloat16), pltpu.SemaphoreType.DMA((3,))],
             compiler_params=params,
         )(col.reshape(1), strip, kernel.reshape(27, CIN, CO))
     with jax.named_scope("edges"):

time: 94.8 us -> 95.6 us (level)
  transfers between devices with their start and end apart: 4 -> 4, of which waited for: 3 -> 2; matrix products, arithmetic and copies ran while one was open for 1% -> 1% of each run, Pallas kernels for 2% -> 3%
where the time goes in v6:
time: 95.6 us; the launch traced here: 95.2 us
  blocking collectives  64.9 us (68%)
  starting transfers between devices  17.5 us (18%)
  local copies, waits for them, and re-layouts  3.94 us (4%)
  waiting for transfers between devices  3.4 us (4%)
  Pallas kernels  2.75 us (3%)
  other arithmetic  1.74 us (2%)
    all_to_all x1, blocking collectives, shards(): shares = lax.all_to_all(local, 'z', 0, 0, tiled=True)  19.4 us
    all_to_all x1, blocking collectives, shards(): lax.all_to_all(jnp.concatenate([rows, xt], axis=1), 'y', 0, 0, tiled=True)  17.2 us
    all_to_all x1, blocking collectives, shards(): lax.all_to_all(jnp.broadcast_to(mine, (16, CHUNK, CO)), TILE, 0, 0, axis_...  14.7 us
    all_to_all x1, blocking collectives, shards(): lax.all_to_all(jnp.broadcast_to(far, (4, 16, CHUNK, CO)), TILE, 0, 0, axi...  13.6 us
    ppermute x1, starting transfers between devices, shards(): pair = lax.ppermute(strip, 'core', swap)  5.38 us
    ppermute x1, starting transfers between devices, shards(): other = lax.ppermute(half, 'core', swap)  4.07 us
    all_to_all x1, starting transfers between devices, shards(): lax.all_to_all(jnp.concatenate([terms, xmine], axis=1), 'x', 0, 0, tiled=...  4.04 us
    ppermute x1, starting transfers between devices, shards(): edge = lax.ppermute(edge, ('z', 'core'), route)  4 us
  transfers between devices with their start and end apart: 4, of which 2 were waited for; matrix products, arithmetic and copies ran while one was open for 1% of the time, Pallas kernels for 3%

profile of v6, /device:TPU:1, one launch (start us, length us, event | category | flops | bytes accessed | tf_op | source)
XLA Modules:
  0.0 95.2 jit_solution(10981776668851862641)
XLA Ops:
  0.6 0.0 copy-start
  0.6 1.0 %copy.16 = bf16[128,64]{0,1:T(8,128)(2,1)S(1)} copy(bf16[128,64]{1,0:T(8,128)(2,1)} %bitcast.44) | data formatting | bytes 32768 | tf_op jit(solution)/shard_map/strip/reshape;strip/squeeze | solution.py:204
  1.6 0.8 broadcast_in_dim.22
  2.4 17.2 %all_to_all.25.g_ref.own_ref = bf16[8,136,128]{2,1,0:T(8,128)(2,1)S(1)} all-to-all(bf16[8,136,128]{2,1,0:T(8,128)(2,1)S(1)} %pad_maximum_fusion.1), channel_id=1, replica_groups=mesh['z'=8,'y'=8,'core'=2,'x'=4] {'y'}, dimensions={0} | all-to-all | bytes 557056 | tf_op jit(solution)/shard_map/strip/all_to_all | solution.py:207
  19.6 5.4 %collective-permute-start = (bf16[8,136,128]{2,1,0:T(8,128)(2,1)S(1)}, bf16[8,136,128]{2,1,0:T(8,128)(2,1)S(1)}, u32[]{:S(2)}, u32[]{:S(2)}) collective-permute-start(bf16[8,136,128]{2,1,0:T(8,128)(2,1)S(1)} %all_to_all.25.g_ref.own_ref), channel_id=1, source_target_pairs={{0,4},{4,0},{1,5},{5,1},{2,6},{6,2},{3,7},{7,3},{8,12},{12,8},{9,1... | collective-permute-start | bytes 835592 | tf_op jit(solution)/shard_map/clips/ppermute | solution.py:209
  25.0 0.0 copy-done
  25.0 1.3 %input_part.1 = bf16[4,160,128]{2,1,0:T(8,128)(2,1)S(1)} custom-call(s32[1]{0:T(128)} %bitcast.6.col_ref, bf16[8,136,128]{2,1,0:T(8,128)(2,1)S(1)} %all_to_all.25.g_ref.own_ref, bf16[27,256,128]{2,1,0:T(8,128)(2,1)S(1)} %bitcast.36), custom_call_target="tpu_custom_call" | custom-call | tf_op jit(solution)/shard_map/input_part/pallas_call | solution.py:211
  26.4 0.0 collective-permute-done.pair_ref
  26.4 0.7 pad_maximum_fusion
  27.2 4.0 %all-to-all-start.1 = ((bf16[4,288,128]{2,1,0:T(8,128)(2,1)}), bf16[4,288,128]{2,1,0:T(8,128)(2,1)S(1)}, u32[]{:S(2)}, u32[]{:S(2)}) async-start(bf16[4,288,128]{2,1,0:T(8,128)(2,1)} %pad_maximum_fusion), calls=%async_computation.1 | async-start | bytes 589824 | tf_op jit(solution)/shard_map/filters/all_to_all | solution.py:228
  31.3 4.0 %collective-permute-start.1 = (bf16[2,8,2,8,128]{4,3,2,1,0:T(8,128)(2,1)S(1)}, bf16[2,8,2,8,128]{4,3,2,1,0:T(8,128)(2,1)S(1)}, u32[]{:S(2)}, u32[]{:S(2)}) collective-permute-start(bf16[2,8,2,8,128]{4,3,2,1,0:T(8,128)(2,1)S(1)} %fusion.2), channel_id=1, source_target_pairs={{64,0},{128,64},{192,128},{256,192},{320,256},{384,320},{448,384},... | collective-permute-start | bytes 196616 | tf_op jit(solution)/shard_map/edges/ppermute | solution.py:224
  35.3 0.1 pad_add_fusion.place_ref
  35.4 2.4 %all-to-all-done.1.got_ref = bf16[4,288,128]{2,1,0:T(8,128)(2,1)S(1)} async-done(((bf16[4,288,128]{2,1,0:T(8,128)(2,1)}), bf16[4,288,128]{2,1,0:T(8,128)(2,1)S(1)}, u32[]{:S(2)}, u32[]{:S(2)}) %all-to-all-start.1) | async-done | bytes 294944 | tf_op jit(solution)/shard_map/filters/all_to_all | solution.py:228
  37.7 1.2 %weight_part.1 = (f32[8,64,128]{2,1,0:T(8,128)S(1)}, f32[64,128]{1,0:T(8,128)S(1)}, bf16[64,128]{1,0:T(8,128)(2,1)S(1)}) custom-call(s32[2]{0:T(128)S(1)} %pad_add_fusion.place_ref, bf16[8,136,128]{2,1,0:T(8,128)(2,1)S(1)} %all_to_all.25.g_ref.own_ref, bf16[8,136,128]{2,1,0:T(8,128)(2,1)S(1)} %collective-permute-done.pair_ref, ...), custom_call_target="tpu_custom_call" | custom-call | tf_op jit(solution)/shard_map/weight_part/pallas_call | solution.py:230
  39.0 0.0 collective-permute-done.1.g_ref
  39.0 0.2 weight_edge.1
  39.2 19.4 %all_to_all.26 = f32[8,64,128]{2,1,0:T(8,128)S(1)} all-to-all(f32[8,64,128]{2,1,0:T(8,128)S(1)} %weight_edge.1), channel_id=1, replica_groups=mesh['z'=8,'y'=8,'core'=2,'x'=4] {'z'}, dimensions={0} | all-to-all | bytes 524288 | tf_op jit(solution)/shard_map/weight_sum/all_to_all | solution.py:252
  58.7 14.7 %all_to_all.27 = bf16[16,56,128]{2,1,0:T(8,128)(2,1)S(1)} all-to-all(bf16[16,56,128]{2,1,0:T(8,128)(2,1)S(1)} %broadcast_in_dim.26), channel_id=1, replica_groups={{0,16,32,48,128,144,160,176,256,272,288,304,384,400,416,432},{4,20,36,5..., dimensions={0} | all-to-all | bytes 458752 | tf_op jit(solution)/shard_map/gather_far/all_to_all | solution.py:256
  73.4 0.1 broadcast_in_dim.27
  73.5 13.6 %all_to_all.28 = bf16[4,16,56,128]{3,2,1,0:T(8,128)(2,1)S(1)} all-to-all(bf16[4,16,56,128]{3,2,1,0:T(8,128)(2,1)S(1)} %broadcast_in_dim.27), channel_id=1, replica_groups={{0,8,64,72},{148,140,84,76},{16,24,80,88},{164,156,100,92},{32,40,96,10..., dimensions={0} | all-to-all | bytes 1835008 | tf_op jit(solution)/shard_map/gather_near/all_to_all | solution.py:260
  87.1 0.2 copy.22
  87.4 4.1 %collective-permute-start.2 = (bf16[14,256,128]{2,1,0:T(8,128)(2,1)S(1)}, bf16[14,256,128]{2,1,0:T(8,128)(2,1)S(1)}, u32[]{:S(2)}, u32[]{:S(2)}) collective-permute-start(bf16[14,256,128]{2,1,0:T(8,128)(2,1)S(1)} %bitcast.38), channel_id=1, source_target_pairs={{0,4},{4,0},{1,5},{5,1},{2,6},{6,2},{3,7},{7,3},{8,12},{12,8},{9,1... | collective-permute-start | bytes 2752520 | tf_op jit(solution)/shard_map/swap/ppermute | solution.py:267
  91.5 0.1 concatenate.28
  91.6 0.1 select_reduce_fusion.1
  91.7 0.1 concatenate.27
  91.8 0.1 concatenate.29
  91.8 0.6 maximum_bitcast_fusion.1
  92.5 1.0 %collective-permute-done.2 = bf16[14,256,128]{2,1,0:T(8,128)(2,1)S(1)} collective-permute-done((bf16[14,256,128]{2,1,0:T(8,128)(2,1)S(1)}, bf16[14,256,128]{2,1,0:T(8,128)(2,1)S(1)}, u32[]{:S(2)}, u32[]{:S(2)}) %collective-permute-start.2) | collective-permute-done | bytes 917536 | tf_op jit(solution)/shard_map/swap/ppermute | solution.py:267
  93.5 0.1 broadcast_select_fusion
  94.0 0.0 copy-start.1
  94.0 1.2 %copy-done.1 = bf16[27,256,128]{2,1,0:T(8,128)(2,1)} copy-done((bf16[27,256,128]{2,1,0:T(8,128)(2,1)}, bf16[27,256,128]{2,1,0:T(8,128)(2,1)S(1)}, u32[]{:S(2)}) %copy-start.1) | copy-done | bytes 1769496
  (27 shorter events, 0.5 us)
Async XLA Ops:
  0.6 24.4 %copy-start = (bf16[3,3,3,256,128]{4,3,2,1,0:T(8,128)(2,1)S(1)}, bf16[3,3,3,256,128]{4,3,2,1,0:T(8,128)(2,1)}, u32[]{:S(2)}) copy-start(bf16[3,3,3,256,128]{4,3,2,1,0:T(8,128)(2,1)} %param.5) | copy-start | bytes 5308420
  19.6 6.8 %collective-permute-start = (bf16[8,136,128]{2,1,0:T(8,128)(2,1)S(1)}, bf16[8,136,128]{2,1,0:T(8,128)(2,1)S(1)}, u32[]{:S(2)}, u32[]{:S(2)}) collective-permute-start(bf16[8,136,128]{2,1,0:T(8,128)(2,1)S(1)} %all_to_all.25.g_ref.own_ref), channel_id=1, source_target_pairs={{0,4},{4,0},{1,5},{5,1},{2,6},{6,2},{3,7},{7,3},{8,12},{12,8},{9,1... | collective-permute-start | bytes 835592 | tf_op jit(solution)/shard_map/clips/ppermute | solution.py:209
  27.2 10.5 %all-to-all-start.1 = ((bf16[4,288,128]{2,1,0:T(8,128)(2,1)}), bf16[4,288,128]{2,1,0:T(8,128)(2,1)S(1)}, u32[]{:S(2)}, u32[]{:S(2)}) async-start(bf16[4,288,128]{2,1,0:T(8,128)(2,1)} %pad_maximum_fusion), calls=%async_computation.1 | async-start | bytes 589824 | tf_op jit(solution)/shard_map/filters/all_to_all | solution.py:228
  31.3 7.7 %collective-permute-start.1 = (bf16[2,8,2,8,128]{4,3,2,1,0:T(8,128)(2,1)S(1)}, bf16[2,8,2,8,128]{4,3,2,1,0:T(8,128)(2,1)S(1)}, u32[]{:S(2)}, u32[]{:S(2)}) collective-permute-start(bf16[2,8,2,8,128]{4,3,2,1,0:T(8,128)(2,1)S(1)} %fusion.2), channel_id=1, source_target_pairs={{64,0},{128,64},{192,128},{256,192},{320,256},{384,320},{448,384},... | collective-permute-start | bytes 196616 | tf_op jit(solution)/shard_map/edges/ppermute | solution.py:224
  87.4 6.2 %collective-permute-start.2 = (bf16[14,256,128]{2,1,0:T(8,128)(2,1)S(1)}, bf16[14,256,128]{2,1,0:T(8,128)(2,1)S(1)}, u32[]{:S(2)}, u32[]{:S(2)}) collective-permute-start(bf16[14,256,128]{2,1,0:T(8,128)(2,1)S(1)} %bitcast.38), channel_id=1, source_target_pairs={{0,4},{4,0},{1,5},{5,1},{2,6},{6,2},{3,7},{7,3},{8,12},{12,8},{9,1... | collective-permute-start | bytes 2752520 | tf_op jit(solution)/shard_map/swap/ppermute | solution.py:267
  94.0 1.2 %copy-start.1 = (bf16[27,256,128]{2,1,0:T(8,128)(2,1)}, bf16[27,256,128]{2,1,0:T(8,128)(2,1)S(1)}, u32[]{:S(2)}) copy-start(bf16[27,256,128]{2,1,0:T(8,128)(2,1)S(1)} %slice_dynamic-update-slice_fusion) | copy-start | bytes 5308420

commit v7 on v5

--- a/solution.py
+++ b/solution.py
@@ -94,15 +94,18 @@
     return prod[:half, CO:], prod[:half, :CO] + prod[half:, CO:], prod[half:, :CO]
 
 
-def weight_kernel(place_ref, own_ref, pair_ref, got_ref, out_ref, inner_ref, edge_ref, mid_ref):
+def weight_kernel(place_ref, own_ref, pair_ref, got_ref, out_ref, edge_ref, mid_ref):
     core, row = place_ref[0], place_ref[1]
     terms = got_ref[:, :TERMS, :].astype(jnp.float32)
-    terms = terms[:, :EXT, :] + terms[:, EXT:, :]
-    terms = (terms[0] + terms[1]) + (terms[2] + terms[3])
-    inner_ref[...] = terms[W : EXT - W]
+
+    def total(start):
+        part = terms[:, start : start + W] + terms[:, EXT + start : EXT + start + W]
+        return (part[0] + part[1]) + (part[2] + part[3])
+
+    above, below = total(0), total(EXT - W)
     for z in range(NZ):
-        up = jnp.where(row - 1 == z, terms[:W], 0.0)
-        out_ref[z, CHUNK:, :] = jnp.where(row + 1 == z, terms[EXT - W :], up)
+        up = jnp.where(row - 1 == z, above, 0.0)
+        out_ref[z, CHUNK:, :] = jnp.where(row + 1 == z, below, up)
 
     x = got_ref[:, TERMS:, :].astype(jnp.float32)
     cell = lax.broadcasted_iota(jnp.int32, x.shape, 2) % (H * W)
@@ -218,15 +221,14 @@
         xmine = jnp.broadcast_to(jnp.concatenate(xmine, axis=0), (NX, NC * NY * CJ, F * H * W))
         got = lax.all_to_all(jnp.concatenate([terms, xmine], axis=1), "x", 0, 0, tiled=True)
     with jax.named_scope("weight_part"):
-        local, inner, outer = pl.pallas_call(
+        local, outer = pl.pallas_call(
             weight_kernel,
             out_shape=[
                 jax.ShapeDtypeStruct((NZ, CHUNK + W, CO), jnp.float32),
-                jax.ShapeDtypeStruct((H * W, F * CI), jnp.float32),
                 jax.ShapeDtypeStruct((F * NX * CJ, NC * NY * W), jnp.bfloat16),
             ],
             in_specs=[smem] + [vmem] * 3,
-            out_specs=[vmem] * 3,
+            out_specs=[vmem] * 2,
             scratch_shapes=[pltpu.VMEM((10, NX * CJ, CO), jnp.float32)],
             compiler_params=params,
         )(jnp.stack([core, row]), strip, pair, got)
@@ -270,7 +272,8 @@
         edges = shares[:, CHUNK:]
         above = jnp.sum(jnp.where(source < row, edges, 0.0), axis=0)
         below = jnp.sum(jnp.where(source > row, edges, 0.0), axis=0)
-        total = inner.reshape(H, W, F * CI)
+        inner = got[:, W : EXT - W].astype(jnp.float32) + got[:, EXT + W : TERMS - W].astype(jnp.float32)
+        total = jnp.sum(inner, axis=0).reshape(H, W, F * CI)
         total = jnp.concatenate([total[:1] + above, total[1:-1], total[-1:] + below], axis=0)
         total = total.astype(jnp.bfloat16).reshape(H, W, F, CI)
         input_grad = jnp.transpose(total, (2, 0, 1, 3))[None]

time: 94.8 us -> 94.7 us (level)
    unnamed x13 -> x14, local copies, waits for them, and re-layouts: 1.42 us -> 2.04 us
where the time goes in v7:
time: 94.7 us; the launch traced here: 94.3 us
  blocking collectives  63.9 us (67%)
  starting transfers between devices  18.2 us (19%)
  local copies, waits for them, and re-layouts  4.54 us (5%)
  waiting for transfers between devices  3.18 us (3%)
  Pallas kernels  2.31 us (2%)
  other arithmetic  1.2 us (1%)
    all_to_all x1, blocking collectives, shards(): shares = lax.all_to_all(local, 'z', 0, 0, tiled=True)  19.1 us
    all_to_all x1, blocking collectives, shards(): lax.all_to_all(jnp.concatenate([rows, xt], axis=1), 'y', 0, 0, tiled=True)  17.2 us
    all_to_all x1, blocking collectives, shards(): lax.all_to_all(jnp.broadcast_to(mine, (16, CHUNK, CO)), TILE, 0, 0, axis_...  14.5 us
    all_to_all x1, blocking collectives, shards(): lax.all_to_all(jnp.broadcast_to(far, (4, 16, CHUNK, CO)), TILE, 0, 0, axi...  13.2 us
    ppermute x1, starting transfers between devices, shards(): pair = lax.ppermute(strip, 'core', swap)  5.38 us
    ppermute x1, starting transfers between devices, shards(): other = lax.ppermute(half, 'core', swap)  4.85 us
    all_to_all x1, starting transfers between devices, shards(): lax.all_to_all(jnp.concatenate([terms, xmine], axis=1), 'x', 0, 0, tiled=...  4.01 us
    ppermute x1, starting transfers between devices, shards(): edge = lax.ppermute(edge, ('z', 'core'), route)  4 us
  transfers between devices with their start and end apart: 4, of which 3 were waited for; matrix products, arithmetic and copies ran while one was open for 1% of the time, Pallas kernels for 2%

profile of v7, /device:TPU:1, one launch (start us, length us, event | category | flops | bytes accessed | tf_op | source)
XLA Modules:
  0.0 94.3 jit_solution(17772853048717409551)
XLA Ops:
  0.6 0.0 copy-start
  0.6 1.0 %copy.11 = bf16[128,64]{0,1:T(8,128)(2,1)S(1)} copy(bf16[128,64]{1,0:T(8,128)(2,1)} %bitcast.44) | data formatting | bytes 32768 | tf_op jit(solution)/shard_map/strip/reshape;strip/squeeze | solution.py:199
  1.6 0.8 broadcast_in_dim.22
  2.4 17.2 %all_to_all.25.g_ref.own_ref = bf16[8,136,128]{2,1,0:T(8,128)(2,1)S(1)} all-to-all(bf16[8,136,128]{2,1,0:T(8,128)(2,1)S(1)} %pad_maximum_fusion.1), channel_id=1, replica_groups=mesh['z'=8,'y'=8,'core'=2,'x'=4] {'y'}, dimensions={0} | all-to-all | bytes 557056 | tf_op jit(solution)/shard_map/strip/all_to_all | solution.py:202
  19.6 5.4 %collective-permute-start = (bf16[8,136,128]{2,1,0:T(8,128)(2,1)S(1)}, bf16[8,136,128]{2,1,0:T(8,128)(2,1)S(1)}, u32[]{:S(2)}, u32[]{:S(2)}) collective-permute-start(bf16[8,136,128]{2,1,0:T(8,128)(2,1)S(1)} %all_to_all.25.g_ref.own_ref), channel_id=1, source_target_pairs={{0,4},{4,0},{1,5},{5,1},{2,6},{6,2},{3,7},{7,3},{8,12},{12,8},{9,1... | collective-permute-start | bytes 835592 | tf_op jit(solution)/shard_map/clips/ppermute | solution.py:204
  25.0 0.0 copy-done
  25.0 0.9 input_part.1
  26.0 0.2 collective-permute-done.pair_ref
  26.2 0.7 pad_maximum_fusion
  26.9 4.0 %all-to-all-start.1 = ((bf16[4,288,128]{2,1,0:T(8,128)(2,1)}), bf16[4,288,128]{2,1,0:T(8,128)(2,1)S(1)}, u32[]{:S(2)}, u32[]{:S(2)}) async-start(bf16[4,288,128]{2,1,0:T(8,128)(2,1)} %pad_maximum_fusion), calls=%async_computation.1 | async-start | bytes 589824 | tf_op jit(solution)/shard_map/filters/all_to_all | solution.py:222
  31.0 4.0 %collective-permute-start.1 = (bf16[2,8,2,8,128]{4,3,2,1,0:T(8,128)(2,1)S(1)}, bf16[2,8,2,8,128]{4,3,2,1,0:T(8,128)(2,1)S(1)}, u32[]{:S(2)}, u32[]{:S(2)}) collective-permute-start(bf16[2,8,2,8,128]{4,3,2,1,0:T(8,128)(2,1)S(1)} %fusion.2), channel_id=1, source_target_pairs={{64,0},{128,64},{192,128},{256,192},{320,256},{384,320},{448,384},... | collective-permute-start | bytes 196616 | tf_op jit(solution)/shard_map/edges/ppermute | solution.py:218
  35.0 0.1 pad_add_fusion.place_ref
  35.1 2.0 %all-to-all-done.1.got_ref = bf16[4,288,128]{2,1,0:T(8,128)(2,1)S(1)} async-done(((bf16[4,288,128]{2,1,0:T(8,128)(2,1)}), bf16[4,288,128]{2,1,0:T(8,128)(2,1)S(1)}, u32[]{:S(2)}, u32[]{:S(2)}) %all-to-all-start.1) | async-done | bytes 294944 | tf_op jit(solution)/shard_map/filters/all_to_all | solution.py:222
  37.1 1.2 %weight_part.1 = (f32[8,64,128]{2,1,0:T(8,128)S(1)}, bf16[64,128]{1,0:T(8,128)(2,1)S(1)}) custom-call(s32[2]{0:T(128)S(1)} %pad_add_fusion.place_ref, bf16[8,136,128]{2,1,0:T(8,128)(2,1)S(1)} %all_to_all.25.g_ref.own_ref, bf16[8,136,128]{2,1,0:T(8,128)(2,1)S(1)} %collective-permute-done.pair_ref, bf16[4,288,128]{2,1,0:T(8,128)(2,1)S(1)} %all-to-all-done.1.got_ref), custom_call_target="tpu_custom_call" | custom-call | tf_op jit(solution)/shard_map/weight_part/pallas_call | solution.py:224
  38.3 0.0 collective-permute-done.1.g_ref
  38.3 0.2 weight_edge.1
  38.5 19.1 %all_to_all.26 = f32[8,64,128]{2,1,0:T(8,128)S(1)} all-to-all(f32[8,64,128]{2,1,0:T(8,128)S(1)} %weight_edge.1), channel_id=1, replica_groups=mesh['z'=8,'y'=8,'core'=2,'x'=4] {'z'}, dimensions={0} | all-to-all | bytes 524288 | tf_op jit(solution)/shard_map/weight_sum/all_to_all | solution.py:245
  57.6 14.5 %all_to_all.27 = bf16[16,56,128]{2,1,0:T(8,128)(2,1)S(1)} all-to-all(bf16[16,56,128]{2,1,0:T(8,128)(2,1)S(1)} %broadcast_in_dim.26), channel_id=1, replica_groups={{0,16,32,48,128,144,160,176,256,272,288,304,384,400,416,432},{4,20,36,5..., dimensions={0} | all-to-all | bytes 458752 | tf_op jit(solution)/shard_map/gather_far/all_to_all | solution.py:249
  72.1 0.1 broadcast_in_dim.27
  72.2 13.2 %all_to_all.28 = bf16[4,16,56,128]{3,2,1,0:T(8,128)(2,1)S(1)} all-to-all(bf16[4,16,56,128]{3,2,1,0:T(8,128)(2,1)S(1)} %broadcast_in_dim.27), channel_id=1, replica_groups={{0,8,64,72},{148,140,84,76},{16,24,80,88},{164,156,100,92},{32,40,96,10..., dimensions={0} | all-to-all | bytes 1835008 | tf_op jit(solution)/shard_map/gather_near/all_to_all | solution.py:253
  85.5 0.2 copy.14
  85.7 4.8 %collective-permute-start.2 = (bf16[14,256,128]{2,1,0:T(8,128)(2,1)S(1)}, bf16[14,256,128]{2,1,0:T(8,128)(2,1)S(1)}, u32[]{:S(2)}, u32[]{:S(2)}) collective-permute-start(bf16[14,256,128]{2,1,0:T(8,128)(2,1)S(1)} %bitcast.38), channel_id=1, source_target_pairs={{0,4},{4,0},{1,5},{5,1},{2,6},{6,2},{3,7},{7,3},{8,12},{12,8},{9,1... | collective-permute-start | bytes 2752520 | tf_op jit(solution)/shard_map/swap/ppermute | solution.py:260
  90.6 0.1 concatenate.28
  90.7 0.1 select_reduce_fusion.1
  90.8 0.1 concatenate.27
  90.9 0.1 concatenate.29
  91.0 0.1 maximum_bitcast_fusion.1
  91.0 0.6 copy.15
  91.6 1.0 %collective-permute-done.2 = bf16[14,256,128]{2,1,0:T(8,128)(2,1)S(1)} collective-permute-done((bf16[14,256,128]{2,1,0:T(8,128)(2,1)S(1)}, bf16[14,256,128]{2,1,0:T(8,128)(2,1)S(1)}, u32[]{:S(2)}, u32[]{:S(2)}) %collective-permute-start.2) | collective-permute-done | bytes 917536 | tf_op jit(solution)/shard_map/swap/ppermute | solution.py:260
  92.6 0.1 broadcast_select_fusion
  93.1 0.0 copy-start.1
  93.1 1.2 %copy-done.1 = bf16[27,256,128]{2,1,0:T(8,128)(2,1)} copy-done((bf16[27,256,128]{2,1,0:T(8,128)(2,1)}, bf16[27,256,128]{2,1,0:T(8,128)(2,1)S(1)}, u32[]{:S(2)}) %copy-start.1) | copy-done | bytes 1769496
  (25 shorter events, 0.5 us)
Async XLA Ops:
  0.6 24.4 %copy-start = (bf16[3,3,3,256,128]{4,3,2,1,0:T(8,128)(2,1)S(1)}, bf16[3,3,3,256,128]{4,3,2,1,0:T(8,128)(2,1)}, u32[]{:S(2)}) copy-start(bf16[3,3,3,256,128]{4,3,2,1,0:T(8,128)(2,1)} %param.5) | copy-start | bytes 5308420
  19.6 6.5 %collective-permute-start = (bf16[8,136,128]{2,1,0:T(8,128)(2,1)S(1)}, bf16[8,136,128]{2,1,0:T(8,128)(2,1)S(1)}, u32[]{:S(2)}, u32[]{:S(2)}) collective-permute-start(bf16[8,136,128]{2,1,0:T(8,128)(2,1)S(1)} %all_to_all.25.g_ref.own_ref), channel_id=1, source_target_pairs={{0,4},{4,0},{1,5},{5,1},{2,6},{6,2},{3,7},{7,3},{8,12},{12,8},{9,1... | collective-permute-start | bytes 835592 | tf_op jit(solution)/shard_map/clips/ppermute | solution.py:204
  26.9 10.2 %all-to-all-start.1 = ((bf16[4,288,128]{2,1,0:T(8,128)(2,1)}), bf16[4,288,128]{2,1,0:T(8,128)(2,1)S(1)}, u32[]{:S(2)}, u32[]{:S(2)}) async-start(bf16[4,288,128]{2,1,0:T(8,128)(2,1)} %pad_maximum_fusion), calls=%async_computation.1 | async-start | bytes 589824 | tf_op jit(solution)/shard_map/filters/all_to_all | solution.py:222
  31.0 7.3 %collective-permute-start.1 = (bf16[2,8,2,8,128]{4,3,2,1,0:T(8,128)(2,1)S(1)}, bf16[2,8,2,8,128]{4,3,2,1,0:T(8,128)(2,1)S(1)}, u32[]{:S(2)}, u32[]{:S(2)}) collective-permute-start(bf16[2,8,2,8,128]{4,3,2,1,0:T(8,128)(2,1)S(1)} %fusion.2), channel_id=1, source_target_pairs={{64,0},{128,64},{192,128},{256,192},{320,256},{384,320},{448,384},... | collective-permute-start | bytes 196616 | tf_op jit(solution)/shard_map/edges/ppermute | solution.py:218
  85.7 6.9 %collective-permute-start.2 = (bf16[14,256,128]{2,1,0:T(8,128)(2,1)S(1)}, bf16[14,256,128]{2,1,0:T(8,128)(2,1)S(1)}, u32[]{:S(2)}, u32[]{:S(2)}) collective-permute-start(bf16[14,256,128]{2,1,0:T(8,128)(2,1)S(1)} %bitcast.38), channel_id=1, source_target_pairs={{0,4},{4,0},{1,5},{5,1},{2,6},{6,2},{3,7},{7,3},{8,12},{12,8},{9,1... | collective-permute-start | bytes 2752520 | tf_op jit(solution)/shard_map/swap/ppermute | solution.py:260
  93.1 1.2 %copy-start.1 = (bf16[27,256,128]{2,1,0:T(8,128)(2,1)}, bf16[27,256,128]{2,1,0:T(8,128)(2,1)S(1)}, u32[]{:S(2)}) copy-start(bf16[27,256,128]{2,1,0:T(8,128)(2,1)S(1)} %slice_dynamic-update-slice_fusion) | copy-start | bytes 5308420
